TPU v7x, 32 devices: a whole 2x2x4 slice. The times are simulated.
32 devices in a mesh: dp: 8 (over y, x, core), seq: 4 (over z).
Axes of the slice: x: 2, y: 2, z: 4, core: 2. Of those that a mesh axis runs over, the one named last changes fastest.
Arguments:
- inputs: bfloat16 [8, 2048, 1472], P('dp', 'seq'), may hold values from -6 to 6
- segments: int32 [8, 2048], P('dp', 'seq'), may hold values from 0 to 5, never falling along the last dimension, each value on 1 to 800 neighbouring positions
- cotangent: bfloat16 [8, 2048, 1472], P('dp', 'seq'), may hold values from -6 to 6
- w_query: bfloat16 [1472, 384], P('dp', 'seq'), may hold values from -0.0546875 to 0.0546875
- w_key: bfloat16 [1472, 384], P('dp', 'seq'), may hold values from -0.109375 to 0.109375
- w_value: bfloat16 [1472, 384], P('dp', 'seq'), may hold values from -0.15625 to 0.15625
- w_out: bfloat16 [384, 1472], P('seq', 'dp'), may hold values from -1.25 to 1.25
- w_gate: bfloat16 [1472, 3584], P('dp', 'seq'), may hold values from -0.15625 to 0.15625
- w_up: bfloat16 [1472, 3584], P('dp', 'seq'), may hold values from -0.15625 to 0.15625
- w_down: bfloat16 [3584, 1472], P('seq', 'dp'), may hold values from -0.1875 to 0.1875
- gain_attn: bfloat16 [1472], P('dp'), may hold values from 0.25 to 1.75
- gain_ffn: bfloat16 [1472], P('dp'), may hold values from 0.25 to 1.75
- rel_table: bfloat16 [32, 6], P('dp'), may hold values from -4 to 4
Outputs:
- outputs: bfloat16 [8, 2048, 1472], P('dp', 'seq')
- input_grad: bfloat16 [8, 2048, 1472], P('dp', 'seq')
- grad_query: float32 [1472, 384], P('dp', 'seq')
- grad_key: float32 [1472, 384], P('dp', 'seq')
- grad_value: float32 [1472, 384], P('dp', 'seq')
- grad_out: float32 [384, 1472], P('seq', 'dp')
- grad_gate: float32 [1472, 3584], P('dp', 'seq')
- grad_up: float32 [1472, 3584], P('dp', 'seq')
- grad_down: float32 [3584, 1472], P('seq', 'dp')
- grad_gain_attn: float32 [1472], P('dp')
- grad_gain_ffn: float32 [1472], P('dp')
- grad_table: float32 [32, 6], P('dp')
Inputs may be any that keep to these rules, and one draw needn't show every extreme that they name: `segments`: along each sequence the ids never fall; each id names one document of 1 to 800 tokens.
All inputs are finite; a program needn't handle non-finite values.
Results may differ from a plain program's by a relative error of at most 0.02.
Values may be sent and summed in bfloat16 or wider, within the bound.
No kernel may reach another device: no remote copies, remote signals or barrier semaphores. Data moves between devices by JAX's collectives and lax.ppermute only.
A program may use at most 256 MiB of HBM per device.

v0:
```python
from functools import partial

import jax
import jax.numpy as jnp
import numpy as np
from jax import lax
from jax.sharding import PartitionSpec as P

HEADS = 6


epsilon = 1e-06
far_steps = np.array([12, 16, 23, 32, 46, 64, 91], np.int32)
masked_score = -1e30
highest = lax.Precision.HIGHEST


def bucket_of(relative):
    distance = jnp.abs(relative)
    levels = jnp.sum(
        (distance[..., None] >= jnp.asarray(far_steps)).astype(jnp.int32), axis=-1, dtype=jnp.int32
    )
    inside = jnp.where(distance < 8, distance, 8 + levels)
    return inside + 16 * (relative > 0).astype(jnp.int32)


def bias_block(lookup, offset, row_count, col_count):
    span_len = row_count + col_count
    positions = jnp.arange(span_len, dtype=jnp.int32)
    shifted = jnp.where(positions < col_count, positions, positions - span_len)
    buckets = bucket_of(offset + shifted)
    one_hot = (buckets[:, None] == jnp.arange(lookup.shape[0], dtype=jnp.int32)[None, :]).astype(
        jnp.float32
    )
    by_distance = jnp.dot(one_hot, lookup, precision=highest).T
    repeated = jnp.tile(by_distance, (1, row_count))[:, : row_count * (span_len - 1)]
    return repeated.reshape(lookup.shape[1], row_count, span_len - 1)[:, :, :col_count]


def rms_norm(tensor, scaling):
    return tensor * lax.rsqrt(jnp.mean(tensor * tensor, axis=-1, keepdims=True) + epsilon) * scaling


def split_blocks(source, block_rows):
    shaped = source.reshape(
        (source.shape[0], source.shape[1] // block_rows, block_rows) + source.shape[2:]
    )
    return jnp.moveaxis(shaped, 1, 0)


def over_blocks(block_fn, block_rows, state, piece):
    pieces = piece[0].shape[1] // block_rows
    starts = block_rows * jnp.arange(pieces, dtype=jnp.int32)
    scan_items = tuple((split_blocks(member, block_rows) for member in piece)) + (starts,)
    state, unused = lax.scan(block_fn, state, scan_items)
    return state


def gather_weights(
    w_query, w_key, w_value, w_out, w_gate, w_up, w_down, gain_attn, gain_ffn, rel_table
):
    seq_query, seq_key, seq_value, seq_out, seq_gate, seq_up, seq_down = (
        lax.all_gather(w_query, "seq", axis=1, tiled=True),
        lax.all_gather(w_key, "seq", axis=1, tiled=True),
        lax.all_gather(w_value, "seq", axis=1, tiled=True),
        lax.all_gather(w_out, "seq", axis=0, tiled=True),
        lax.all_gather(w_gate, "seq", axis=1, tiled=True),
        lax.all_gather(w_up, "seq", axis=1, tiled=True),
        lax.all_gather(w_down, "seq", axis=0, tiled=True),
    )
    return (
        lax.all_gather(seq_query, "dp", axis=0, tiled=True),
        lax.all_gather(seq_key, "dp", axis=0, tiled=True),
        lax.all_gather(seq_value, "dp", axis=0, tiled=True),
        lax.all_gather(seq_out, "dp", axis=1, tiled=True),
        lax.all_gather(seq_gate, "dp", axis=0, tiled=True),
        lax.all_gather(seq_up, "dp", axis=0, tiled=True),
        lax.all_gather(seq_down, "dp", axis=1, tiled=True),
        lax.all_gather(gain_attn, "dp", axis=0, tiled=True),
        lax.all_gather(gain_ffn, "dp", axis=0, tiled=True),
        lax.all_gather(rel_table, "dp", axis=0, tiled=True),
    )


def on_device(
    inputs,
    segments,
    cotangent,
    w_query,
    w_key,
    w_value,
    w_out,
    w_gate,
    w_up,
    w_down,
    gain_attn,
    gain_ffn,
    rel_table,
):
    (
        full_query,
        full_key,
        full_value,
        full_out,
        full_gate,
        full_up,
        full_down,
        full_gain_attn,
        full_gain_ffn,
        full_table,
    ) = gather_weights(
        w_query, w_key, w_value, w_out, w_gate, w_up, w_down, gain_attn, gain_ffn, rel_table
    )
    seq_count, tok_rows, model_dim = inputs.shape
    inner_dim = full_query.shape[1]
    head_size = inner_dim // HEADS
    tok_total = seq_count * tok_rows
    gain_one = full_gain_attn.astype(jnp.float32)
    gain_two = full_gain_ffn.astype(jnp.float32)
    table_full = full_table.astype(jnp.float32)
    source = inputs.reshape(tok_total, model_dim).astype(jnp.float32)
    normed_float, norm_one_pull = jax.vjp(rms_norm, source, gain_one)
    normed_one = normed_float.astype(jnp.bfloat16)
    query_rows = jnp.dot(normed_one, full_query, preferred_element_type=jnp.float32).astype(
        jnp.bfloat16
    )
    key_rows = jnp.dot(normed_one, full_key, preferred_element_type=jnp.float32).astype(
        jnp.bfloat16
    )
    value_rows = jnp.dot(normed_one, full_value, preferred_element_type=jnp.float32).astype(
        jnp.bfloat16
    )
    query_four = query_rows.reshape(seq_count, tok_rows, HEADS, head_size)
    key_shard = key_rows.reshape(seq_count, tok_rows, inner_dim)
    value_shard = value_rows.reshape(seq_count, tok_rows, inner_dim)
    my_keys_four = key_rows.reshape(seq_count, tok_rows, HEADS, head_size)
    my_values_four = value_rows.reshape(seq_count, tok_rows, HEADS, head_size)
    first_pos = lax.axis_index("seq") * tok_rows

    def masked_scores(key_block, key_segs, bias_part):
        keys_four = key_block.reshape(seq_count, tok_rows, HEADS, head_size)
        scores = jnp.einsum(
            "sqhe,skhe->shqk", query_four, keys_four, preferred_element_type=jnp.float32
        )
        scores = scores + bias_part[None]
        same_doc = segments[:, None, :, None] == key_segs[:, None, None, :]
        return jnp.where(same_doc, scores, masked_score)

    def forward_block(state, block_item):
        key_block, value_block, key_segs, key_start = block_item
        peak_old, total_old, summed_old = state
        bias_part = bias_block(table_full, key_start - first_pos, tok_rows, tok_rows)
        scores = masked_scores(key_block, key_segs, bias_part)
        peak_new = jnp.maximum(peak_old, jnp.max(scores, axis=3))
        fading = jnp.exp(peak_old - peak_new)
        weights = jnp.exp(scores - peak_new[..., None])
        total_new = total_old * fading + jnp.sum(weights, axis=3)
        values_four = value_block.reshape(seq_count, tok_rows, HEADS, head_size)
        summed_new = summed_old * fading[..., None] + jnp.einsum(
            "shqk,skhe->shqe",
            weights.astype(jnp.bfloat16),
            values_four,
            preferred_element_type=jnp.float32,
        )
        state = (peak_new, total_new, summed_new)
        return (state, None)

    stat_shape = (seq_count, HEADS, tok_rows)
    start_state = (
        jnp.full(stat_shape, masked_score, jnp.float32),
        jnp.zeros(stat_shape, jnp.float32),
        jnp.zeros(stat_shape + (head_size,), jnp.float32),
    )
    peak_all, total_all, summed = over_blocks(
        forward_block,
        tok_rows,
        start_state,
        (
            lax.all_gather(key_shard, "seq", axis=1, tiled=True),
            lax.all_gather(value_shard, "seq", axis=1, tiled=True),
            lax.all_gather(segments, "seq", axis=1, tiled=True),
        ),
    )
    attn_out = summed / total_all[..., None]
    log_total = peak_all + jnp.log(total_all)
    attended = (
        jnp.transpose(attn_out, (0, 2, 1, 3)).reshape(tok_total, inner_dim).astype(jnp.bfloat16)
    )
    mixed = source + jnp.dot(attended, full_out, preferred_element_type=jnp.float32)
    normed_two_float, norm_two_pull = jax.vjp(rms_norm, mixed, gain_two)
    normed_two = normed_two_float.astype(jnp.bfloat16)
    gate_rows = jnp.dot(normed_two, full_gate, preferred_element_type=jnp.float32)
    up_rows = jnp.dot(normed_two, full_up, preferred_element_type=jnp.float32)
    gelu_out, gelu_pull = jax.vjp(partial(jax.nn.gelu, approximate=True), gate_rows)
    hidden = (gelu_out * up_rows).astype(jnp.bfloat16)
    outputs = (mixed + jnp.dot(hidden, full_down, preferred_element_type=jnp.float32)).astype(
        jnp.bfloat16
    )
    (
        full_query,
        full_key,
        full_value,
        full_out,
        full_gate,
        full_up,
        full_down,
        full_gain_attn,
        full_gain_ffn,
        full_table,
    ) = gather_weights(
        w_query, w_key, w_value, w_out, w_gate, w_up, w_down, gain_attn, gain_ffn, rel_table
    )
    table_full = full_table.astype(jnp.float32)
    tangent = cotangent.reshape(tok_total, model_dim)
    grad_hidden = jnp.dot(tangent, full_down.T, preferred_element_type=jnp.float32)
    grad_gate_rows = gelu_pull(grad_hidden * up_rows)[0].astype(jnp.bfloat16)
    grad_up_rows = (grad_hidden * gelu_out).astype(jnp.bfloat16)
    grad_normed_two = jnp.dot(
        grad_gate_rows, full_gate.T, preferred_element_type=jnp.float32
    ) + jnp.dot(grad_up_rows, full_up.T, preferred_element_type=jnp.float32)
    grad_mixed, grad_gain_ffn = norm_two_pull(grad_normed_two)
    grad_mixed = grad_mixed + tangent.astype(jnp.float32)
    grad_branch = grad_mixed.astype(jnp.bfloat16)
    grad_attended = jnp.dot(grad_branch, full_out.T, preferred_element_type=jnp.float32).astype(
        jnp.bfloat16
    )
    grad_four = grad_attended.reshape(seq_count, tok_rows, HEADS, head_size)
    row_delta = jnp.einsum(
        "sqhe,shqe->shq", grad_four.astype(jnp.float32), attn_out, precision=highest
    )

    def backward_block(state, block_item):
        key_block, value_block, key_segs, key_start = block_item

        def backward_compute(current):
            grad_query_acc, grad_lookup = current

            def place_bias(lookup):
                return bias_block(lookup, key_start - first_pos, tok_rows, tok_rows)

            bias_part, bias_pull = jax.vjp(place_bias, table_full)
            scores = masked_scores(key_block, key_segs, bias_part)
            probs = jnp.exp(scores - log_total[..., None])
            keys_four = key_block.reshape(seq_count, tok_rows, HEADS, head_size)
            values_four = value_block.reshape(seq_count, tok_rows, HEADS, head_size)
            grad_probs = jnp.einsum(
                "sqhe,skhe->shqk", grad_four, values_four, preferred_element_type=jnp.float32
            )
            grad_scores = probs * (grad_probs - row_delta[..., None])
            grad_lookup = grad_lookup + bias_pull(jnp.sum(grad_scores, axis=0))[0]
            grad_query_acc = grad_query_acc + jnp.einsum(
                "shqk,skhe->shqe",
                grad_scores.astype(jnp.bfloat16),
                keys_four,
                preferred_element_type=jnp.float32,
            )
            return (grad_query_acc, grad_lookup)

        state = backward_compute(state)
        return (state, None)

    grad_start = (
        jnp.zeros(stat_shape + (head_size,), jnp.float32),
        jnp.zeros(table_full.shape, jnp.float32),
    )
    grad_query_acc, grad_lookup = over_blocks(
        backward_block,
        tok_rows,
        grad_start,
        (
            lax.all_gather(key_shard, "seq", axis=1, tiled=True),
            lax.all_gather(value_shard, "seq", axis=1, tiled=True),
            lax.all_gather(segments, "seq", axis=1, tiled=True),
        ),
    )

    def query_side_block(state, block_item):
        query_block, answer_block, total_block, delta_block, query_segs, query_start = block_item
        bias_part = bias_block(table_full, first_pos - query_start, tok_rows, tok_rows)
        other_query = query_block.astype(jnp.bfloat16).reshape(
            seq_count, tok_rows, HEADS, head_size
        )
        other_answer = answer_block.astype(jnp.bfloat16).reshape(
            seq_count, tok_rows, HEADS, head_size
        )
        scores = (
            jnp.einsum(
                "sqhe,skhe->shqk", other_query, my_keys_four, preferred_element_type=jnp.float32
            )
            + bias_part[None]
        )
        same_doc = query_segs[:, None, :, None] == segments[:, None, None, :]
        scores = jnp.where(same_doc, scores, masked_score)
        probs = jnp.exp(scores - jnp.transpose(total_block, (0, 2, 1))[..., None])
        grad_probs = jnp.einsum(
            "sqhe,skhe->shqk", other_answer, my_values_four, preferred_element_type=jnp.float32
        )
        grad_scores = probs * (grad_probs - jnp.transpose(delta_block, (0, 2, 1))[..., None])
        grad_keys = jnp.einsum(
            "shqk,sqhe->skhe",
            grad_scores.astype(jnp.bfloat16),
            other_query,
            preferred_element_type=jnp.float32,
        ).reshape(seq_count, tok_rows, inner_dim)
        grad_values = jnp.einsum(
            "shqk,sqhe->skhe",
            probs.astype(jnp.bfloat16),
            other_answer,
            preferred_element_type=jnp.float32,
        ).reshape(seq_count, tok_rows, inner_dim)
        state = state + jnp.concatenate([grad_keys, grad_values], axis=2)
        return (state, None)

    query_send = query_rows.reshape(seq_count, tok_rows, inner_dim).astype(jnp.float32)
    answer_send = grad_attended.reshape(seq_count, tok_rows, inner_dim).astype(jnp.float32)
    total_send = jnp.transpose(log_total, (0, 2, 1))
    delta_send = jnp.transpose(row_delta, (0, 2, 1))
    pair_start = jnp.zeros((seq_count, tok_rows, 2 * inner_dim), jnp.float32)
    own_pairs = over_blocks(
        query_side_block,
        tok_rows,
        pair_start,
        (
            lax.all_gather(query_send, "seq", axis=1, tiled=True),
            lax.all_gather(answer_send, "seq", axis=1, tiled=True),
            lax.all_gather(total_send, "seq", axis=1, tiled=True),
            lax.all_gather(delta_send, "seq", axis=1, tiled=True),
            lax.all_gather(segments, "seq", axis=1, tiled=True),
        ),
    )
    grad_query_low = (
        jnp.transpose(grad_query_acc, (0, 2, 1, 3))
        .reshape(tok_total, inner_dim)
        .astype(jnp.bfloat16)
    )
    grad_key_low = own_pairs[:, :, :inner_dim].reshape(tok_total, inner_dim).astype(jnp.bfloat16)
    grad_value_low = own_pairs[:, :, inner_dim:].reshape(tok_total, inner_dim).astype(jnp.bfloat16)
    grad_normed = (
        jnp.dot(grad_query_low, full_query.T, preferred_element_type=jnp.float32)
        + jnp.dot(grad_key_low, full_key.T, preferred_element_type=jnp.float32)
        + jnp.dot(grad_value_low, full_value.T, preferred_element_type=jnp.float32)
    )
    grad_source, grad_gain_attn = norm_one_pull(grad_normed)
    input_grad = (
        (grad_mixed + grad_source).astype(jnp.bfloat16).reshape(seq_count, tok_rows, model_dim)
    )
    normed_all, normed_two_all, tangent_all, branch_all = (
        lax.all_gather(normed_one, "seq", axis=0, tiled=True),
        lax.all_gather(normed_two, "seq", axis=0, tiled=True),
        lax.all_gather(tangent, "seq", axis=0, tiled=True),
        lax.all_gather(grad_branch, "seq", axis=0, tiled=True),
    )
    query_cols, key_cols, value_cols, attended_cols, hidden_cols, gate_cols, up_cols = (
        lax.all_to_all(grad_query_low, "seq", split_axis=1, concat_axis=0, tiled=True),
        lax.all_to_all(grad_key_low, "seq", split_axis=1, concat_axis=0, tiled=True),
        lax.all_to_all(grad_value_low, "seq", split_axis=1, concat_axis=0, tiled=True),
        lax.all_to_all(attended, "seq", split_axis=1, concat_axis=0, tiled=True),
        lax.all_to_all(hidden, "seq", split_axis=1, concat_axis=0, tiled=True),
        lax.all_to_all(grad_gate_rows, "seq", split_axis=1, concat_axis=0, tiled=True),
        lax.all_to_all(grad_up_rows, "seq", split_axis=1, concat_axis=0, tiled=True),
    )
    grad_query = jnp.dot(normed_all.T, query_cols, preferred_element_type=jnp.float32)
    grad_key = jnp.dot(normed_all.T, key_cols, preferred_element_type=jnp.float32)
    grad_value = jnp.dot(normed_all.T, value_cols, preferred_element_type=jnp.float32)
    grad_out = jnp.dot(attended_cols.T, branch_all, preferred_element_type=jnp.float32)
    grad_gate = jnp.dot(normed_two_all.T, gate_cols, preferred_element_type=jnp.float32)
    grad_up = jnp.dot(normed_two_all.T, up_cols, preferred_element_type=jnp.float32)
    grad_down = jnp.dot(hidden_cols.T, tangent_all, preferred_element_type=jnp.float32)
    (
        own_query,
        own_key,
        own_value,
        own_out,
        own_gate,
        own_up,
        own_down,
        part_gain_attn,
        part_gain_ffn,
        part_lookup,
    ) = (
        lax.psum_scatter(grad_query, "dp", scatter_dimension=0, tiled=True),
        lax.psum_scatter(grad_key, "dp", scatter_dimension=0, tiled=True),
        lax.psum_scatter(grad_value, "dp", scatter_dimension=0, tiled=True),
        lax.psum_scatter(grad_out, "dp", scatter_dimension=1, tiled=True),
        lax.psum_scatter(grad_gate, "dp", scatter_dimension=0, tiled=True),
        lax.psum_scatter(grad_up, "dp", scatter_dimension=0, tiled=True),
        lax.psum_scatter(grad_down, "dp", scatter_dimension=1, tiled=True),
        lax.psum_scatter(grad_gain_attn, "dp", scatter_dimension=0, tiled=True),
        lax.psum_scatter(grad_gain_ffn, "dp", scatter_dimension=0, tiled=True),
        lax.psum_scatter(grad_lookup, "dp", scatter_dimension=0, tiled=True),
    )
    own_gain_attn, own_gain_ffn, own_lookup = lax.psum(
        (part_gain_attn, part_gain_ffn, part_lookup), "seq"
    )
    return (
        outputs.reshape(seq_count, tok_rows, model_dim),
        input_grad,
        own_query,
        own_key,
        own_value,
        own_out,
        own_gate,
        own_up,
        own_down,
        own_gain_attn,
        own_gain_ffn,
        own_lookup,
    )


def solution(mesh):
    return jax.shard_map(
        on_device,
        mesh=mesh,
        in_specs=(
            P("dp", "seq", None),
            P("dp", "seq"),
            P("dp", "seq", None),
            P("dp", "seq"),
            P("dp", "seq"),
            P("dp", "seq"),
            P("seq", "dp"),
            P("dp", "seq"),
            P("dp", "seq"),
            P("seq", "dp"),
            P("dp"),
            P("dp"),
            P("dp", None),
        ),
        out_specs=(
            P("dp", "seq", None),
            P("dp", "seq", None),
            P("dp", "seq"),
            P("dp", "seq"),
            P("dp", "seq"),
            P("seq", "dp"),
            P("dp", "seq"),
            P("dp", "seq"),
            P("seq", "dp"),
            P("dp"),
            P("dp"),
            P("dp", None),
        ),
        check_vma=False,
    )
```

profile of v0, /device:TPU:10, one launch (start us, length us, event | category | flops | bytes accessed | tf_op | source)
XLA Modules:
  0.0 2181.7 jit_solution(1407496684638721311)
XLA Ops:
  7.3 14.6 all-gather.5
  77.2 14.8 all-gather.9
  93.0 16.6 all-gather.37.cloned.1.call-done
  109.7 32.8 %all-gather.41.cloned.1.call-done = bf16[184,3584]{1,0:T(8,128)(2,1)} async-done(((bf16[184,896]{1,0:T(8,128)(2,1)}), bf16[184,3584]{1,0:T(8,128)(2,1)}) %all-gather.41.cloned.1.call-update) | async-done | bytes 1318928 | tf_op jit(solution)/shard_map/all_gather | solution.py:68
  142.5 33.2 %all-gather.45.cloned.1.call-done = bf16[3584,184]{0,1:T(8,128)(2,1)} async-done(((bf16[896,184]{0,1:T(8,128)(2,1)}), bf16[3584,184]{0,1:T(8,128)(2,1)}) %all-gather.45.cloned.1.call-update) | async-done | bytes 1318928 | tf_op jit(solution)/shard_map/all_gather | solution.py:69
  204.4 35.3 %all-gather.55.cloned.1.call-done = bf16[2048,384]{0,1:T(8,128)(2,1)} async-done(((bf16[512,384]{0,1:T(8,128)(2,1)}), bf16[2048,384]{0,1:T(8,128)(2,1)}) %all-gather.55.cloned.1.call-update) | async-done | bytes 1572880 | tf_op jit(solution)/shard_map/all_gather | solution.py:179
  244.1 33.8 %all-gather.57.cloned.1.call-done = bf16[2048,384]{0,1:T(8,128)(2,1)} async-done(((bf16[512,384]{0,1:T(8,128)(2,1)}), bf16[2048,384]{0,1:T(8,128)(2,1)}) %all-gather.57.cloned.1.call-update) | async-done | bytes 1572880 | tf_op jit(solution)/shard_map/all_gather | solution.py:180
  284.6 385.0 %while.48 = (s32[]{:T(128)}, f32[1,6,512]{2,1,0:T(8,128)S(1)}, f32[1,6,512]{2,1,0:T(8,128)S(1)}, f32[1,6,512,64]{2,3,1,0:T(8,128)S(1)}, s32[1,512]{1,0:T(1,128)}...) while((s32[]{:T(128)}, f32[1,6,512]{2,1,0:T(8,128)S(1)}, ...), condition=%wide.region_5.6_spmd.clone.clone, body=%wide.region_1.5_spmd.sunk.clone.clone.sunk | while | flops 416962560 | bytes 193799184 | solution.py:55
  305.3 17.9 copy.162
  348.6 14.2 reshape.729
  399.4 19.0 copy.162
  442.4 14.7 reshape.729
  493.7 18.1 copy.162
  585.6 17.9 copy.162
  697.2 19.2 multiply_convert_fusion.2
  747.5 14.5 all_gather.124
  772.9 670.0 %while.49 = (s32[]{:T(128)}, f32[1,6,512,64]{2,3,1,0:T(8,128)S(1)}, f32[32,6]{0,1:T(8,128)S(1)}, s32[1,512]{1,0:T(1,128)}, s32[4,1,512]{2,1,0:T(1,128)S(1)}, /*i...) while((s32[]{:T(128)}, f32[1,6,512,64]{2,3,1,0:T(8,128)S(1)}, ...), condition=%wide.region_11.12_spmd.clone.clone, body=%wide.region_8.11_spmd.sunk.clone.clone.sunk | while | flops 622033280 | bytes 320223744 | solution.py:55
  804.3 17.9 copy.165
  846.0 14.1 reshape.731
  962.8 18.0 copy.165
  1121.5 18.3 copy.165
  1163.6 14.1 reshape.731
  1280.2 17.9 copy.165
  1465.7 331.1 %while.50 = (s32[]{:T(128)}, f32[1,512,768]{1,2,0:T(8,128)}, bf16[4,1,512,384]{2,0,3,1:T(4,128)(2,1)}, s32[4,1,512]{2,1,0:T(1,128)S(1)}, s32[1,512]{1,0:T(1,128)...) while((s32[]{:T(128)}, f32[1,512,768]{1,2,0:T(8,128)}, ...), condition=%wide.region_14.15_spmd.clone.clone, body=%wide.region_12.14_spmd.sunk.clone.clone.sunk | while | flops 820187136 | bytes 175981568 | solution.py:55
  1477.3 17.9 copy.169
  1558.9 17.9 copy.169
  1641.9 17.9 copy.169
  1724.9 17.9 copy.169
  1854.0 47.3 %all-to-all-done.4 = bf16[512,4,896]{2,0,1:T(8,128)(2,1)} async-done(((bf16[512,4,896]{2,0,1:T(8,128)(2,1)}), bf16[512,4,896]{2,0,1:T(8,128)(2,1)}, u32[]{:S(2)}, u32[]{:S(2)}) %all-to-all-start.4) | async-done | bytes 3670048 | tf_op jit(solution)/shard_map/all_to_all | solution.py:359
  1914.8 85.9 %all_to_all.122 = bf16[512,4,896]{2,0,1:T(8,128)(2,1)S(1)} all-to-all(bf16[512,4,896]{2,0,1:T(8,128)(2,1)S(1)} %bitcast.421), channel_id=1, replica_groups=mesh['dp'=8,'seq'=4] {'seq'}, dimensions={1} | all-to-all | bytes 7340032 | tf_op jit(solution)/shard_map/all_to_all | solution.py:360
  2019.6 77.7 %all-to-all-done.6 = bf16[512,4,896]{2,0,1:T(8,128)(2,1)} async-done(((bf16[512,4,896]{2,0,1:T(8,128)(2,1)}), bf16[512,4,896]{2,0,1:T(8,128)(2,1)}, u32[]{:S(2)}, u32[]{:S(2)}) %all-to-all-start.6) | async-done | bytes 3670048 | tf_op jit(solution)/shard_map/all_to_all | solution.py:358
  2127.9 20.6 all-reduce.14
  (515 shorter events, 1386.4 us)
Async XLA Ops:
  7.2 60.6 %all-gather.29.cloned.1.call-start = ((), (), s32[]{:S(2)}) async-start(), calls=%async_computation.14 | async-start | bytes 1271808 | tf_op jit(solution)/shard_map/all_gather | solution.py:73
  22.8 51.5 %all-gather.33.cloned.1.call-start = ((), (), s32[]{:S(2)}) async-start(), calls=%async_computation.16 | async-start | bytes 1271808 | tf_op jit(solution)/shard_map/all_gather | solution.py:74
  37.6 72.0 %all-gather.37.cloned.1.call-start = ((), (), s32[]{:S(2)}) async-start(), calls=%async_computation.18 | async-start | bytes 1648640 | tf_op jit(solution)/shard_map/all_gather | solution.py:67
  38.3 104.1 %all-gather.41.cloned.1.call-start = ((), (), s32[]{:S(2)}) async-start(), calls=%async_computation.20 | async-start | bytes 1648640 | tf_op jit(solution)/shard_map/all_gather | solution.py:68
  38.9 136.8 %all-gather.45.cloned.1.call-start = ((), (), s32[]{:S(2)}) async-start(), calls=%async_computation.22 | async-start | bytes 1648640 | tf_op jit(solution)/shard_map/all_gather | solution.py:69
  39.5 162.0 %all-gather.31.cloned.1.call-start = ((), (), s32[]{:S(2)}) async-start(), calls=%async_computation.15 | async-start | bytes 1271808 | tf_op jit(solution)/shard_map/all_gather | solution.py:72
  54.3 185.4 %all-gather.55.cloned.1.call-start = ((), (), s32[]{:S(2)}) async-start(), calls=%async_computation.27 | async-start | bytes 1966080 | tf_op jit(solution)/shard_map/all_gather | solution.py:179
  67.8 133.7 %copy-start.15 = (bf16[512,1472]{0,1:T(8,128)(2,1)}, bf16[512,1472]{0,1:T(8,128)(2,1)S(1)}, u32[]{:S(2)}) copy-start(bf16[512,1472]{0,1:T(8,128)(2,1)S(1)} %fusion.67) | copy-start | bytes 4521988
  71.2 206.7 %all-gather.57.cloned.1.call-start = ((), (), s32[]{:S(2)}) async-start(), calls=%async_computation.28 | async-start | bytes 1966080 | tf_op jit(solution)/shard_map/all_gather | solution.py:180
  77.1 98.7 %copy-start.39 = (bf16[4,6]{1,0:T(4,128)(2,1)S(1)}, bf16[4,6]{1,0:T(4,128)(2,1)}, u32[]{:S(2)}) copy-start(bf16[4,6]{1,0:T(4,128)(2,1)} %param.32) | copy-start | bytes 148
  77.2 593.5 %all-gather.35.cloned.1.call-start = ((), (), s32[]{:S(2)}) async-start(), calls=%async_computation.17 | async-start | bytes 1271808 | tf_op jit(solution)/shard_map/all_gather | solution.py:75
  93.0 582.3 %all-gather.39.cloned.1.call-start = ((), (), s32[]{:S(2)}) async-start(), calls=%async_computation.19 | async-start | bytes 11870208 | tf_op jit(solution)/shard_map/all_gather | solution.py:76
  109.6 576.6 %all-gather.43.cloned.1.call-start = ((), (), s32[]{:S(2)}) async-start(), calls=%async_computation.21 | async-start | bytes 11870208 | tf_op jit(solution)/shard_map/all_gather | solution.py:77
  142.5 554.8 %all-gather.47.cloned.1.call-start = ((), (), s32[]{:S(2)}) async-start(), calls=%async_computation.23 | async-start | bytes 11870208 | tf_op jit(solution)/shard_map/all_gather | solution.py:78
  175.8 593.1 %all-gather.59.cloned.1.call-start = ((), (), s32[]{:S(2)}) async-start(), calls=%async_computation.29 | async-start | bytes 1966080 | tf_op jit(solution)/shard_map/all_gather | solution.py:324
  204.4 1252.3 %all-gather.61.cloned.1.call-start = ((), (), s32[]{:S(2)}) async-start(), calls=%async_computation.30 | async-start | bytes 1966080 | tf_op jit(solution)/shard_map/all_gather | solution.py:325
  744.6 1086.4 %all-gather.49.cloned.1.call-start = ((), (), s32[]{:S(2)}) async-start(), calls=%async_computation.24 | async-start | bytes 7536640 | tf_op jit(solution)/shard_map/all_gather | solution.py:348
  745.1 1103.3 %all-gather.51.cloned.1.call-start = ((), (), s32[]{:S(2)}) async-start(), calls=%async_computation.25 | async-start | bytes 7536640 | tf_op jit(solution)/shard_map/all_gather | solution.py:351
  745.7 1108.2 %all-gather.53.cloned.1.call-start = ((), (), s32[]{:S(2)}) async-start(), calls=%async_computation.26 | async-start | bytes 7536640 | tf_op jit(solution)/shard_map/all_gather | solution.py:349
  746.3 1273.3 %all-gather.63.cloned.1.call-start = ((), (), s32[]{:S(2)}) async-start(), calls=%async_computation.31 | async-start | bytes 7536640 | tf_op jit(solution)/shard_map/all_gather | solution.py:350
  762.1 698.5 %all-to-all-start.3 = ((bf16[512,4,96]{0,2,1:T(8,128)(2,1)}), bf16[512,4,96]{0,2,1:T(8,128)(2,1)}, u32[]{:S(2)}, u32[]{:S(2)}) async-start(bf16[512,4,96]{0,2,1:T(8,128)(2,1)} %bitcast.46), calls=%async_computation.3 | async-start | bytes 786432 | tf_op jit(solution)/shard_map/all_to_all | solution.py:357
  1460.5 338.4 %all-to-all-start = ((bf16[512,4,96]{0,2,1:T(8,128)(2,1)}), bf16[512,4,96]{0,2,1:T(8,128)(2,1)}, u32[]{:S(2)}, u32[]{:S(2)}) async-start(bf16[512,4,96]{0,2,1:T(8,128)(2,1)} %bitcast.40), calls=%async_computation | async-start | bytes 786432 | tf_op jit(solution)/shard_map/all_to_all | solution.py:354
  1811.1 12.6 all-to-all-start.2
  1823.7 77.6 %all-to-all-start.4 = ((bf16[512,4,896]{2,0,1:T(8,128)(2,1)}), bf16[512,4,896]{2,0,1:T(8,128)(2,1)}, u32[]{:S(2)}, u32[]{:S(2)}) async-start(bf16[512,4,896]{2,0,1:T(8,128)(2,1)} %bitcast.419), calls=%async_computation.4 | async-start | bytes 7340032 | tf_op jit(solution)/shard_map/all_to_all | solution.py:359
  1829.9 337.9 %reduce-scatter.22.cloned.1.call-start = ((), (), s32[]{:S(2)}) async-start(), calls=%async_computation.32 | async-start | bytes 847872
  1836.3 331.5 %reduce-scatter.24.cloned.1.call-start = ((), (), s32[]{:S(2)}) async-start(), calls=%async_computation.33 | async-start | bytes 847872
  1841.8 326.0 %reduce-scatter.26.cloned.1.call-start = ((), (), s32[]{:S(2)}) async-start(), calls=%async_computation.34 | async-start | bytes 847872
  1847.3 320.4 %reduce-scatter.28.cloned.1.call-start = ((), (), s32[]{:S(2)}) async-start(), calls=%async_computation.35 | async-start | bytes 847872
  1853.9 313.9 %reduce-scatter.30.cloned.1.call-start = ((), (), s32[]{:S(2)}) async-start(), calls=%async_computation.36 | async-start | bytes 5935104
  1912.3 255.6 %reduce-scatter.32.cloned.1.call-start = ((), (), s32[]{:S(2)}) async-start(), calls=%async_computation.37 | async-start | bytes 5935104
  2013.0 84.3 %all-to-all-start.6 = ((bf16[512,4,896]{2,0,1:T(8,128)(2,1)}), bf16[512,4,896]{2,0,1:T(8,128)(2,1)}, u32[]{:S(2)}, u32[]{:S(2)}) async-start(bf16[512,4,896]{2,0,1:T(8,128)(2,1)} %bitcast.420), calls=%async_computation.6 | async-start | bytes 7340032 | tf_op jit(solution)/shard_map/all_to_all | solution.py:358
  2019.6 155.4 %reduce-scatter.34.cloned.1.call-start = ((), (), s32[]{:S(2)}) async-start(), calls=%async_computation.38 | async-start | bytes 5935104
  (51 other events, 987.9 us)
Sparse Core Ops, SparseCore 0:
  22.9 24.8 all-gather.28
  50.2 24.0 all-gather.32
  75.9 33.6 all-gather.36
  111.1 31.3 all-gather.40
  143.9 31.8 all-gather.44
  178.1 23.4 all-gather.30
  203.7 36.0 all-gather.54
  241.9 35.9 all-gather.56
  280.4 23.7 all-gather.34
  305.9 63.5 all-gather.38
  371.3 63.5 all-gather.42
  436.6 63.5 all-gather.46
  502.3 36.0 all-gather.58
  744.7 43.2 all-gather.60
  789.3 110.2 all-gather.48
  901.7 109.2 all-gather.50
  1013.0 109.2 all-gather.52
  1123.7 109.2 all-gather.62
  1836.4 34.8 reduce-scatter.21
  1875.0 34.1 reduce-scatter.23
  1913.1 34.1 reduce-scatter.25
  1951.2 34.1 reduce-scatter.27
  1989.3 59.0 reduce-scatter.29
  2052.6 59.0 reduce-scatter.31
  2115.7 59.2 reduce-scatter.33
where the time goes:
time: 2200 us; the launch traced here: 2180 us
  local copies, waits for them, and re-layouts  1160 us (53%)
  waiting for transfers between devices  300 us (14%)
  matrix products  263 us (12%)
  blocking collectives  246 us (11%)
  other arithmetic  102 us (5%)
  loops' own time  57.9 us (3%)
  starting transfers between devices  30.7 us (1%)
    while x80, local copies, waits for them, and re-layouts  588 us
    reshape x16, local copies, waits for them, and re-layouts, bias_block(): repeated.reshape(lookup.shape[1], row_count, span_len - 1)[:, :, :col_count]  226 us
    slice x12, local copies, waits for them, and re-layouts, bias_block(): jnp.tile(by_distance, (1, row_count))[:, :row_count * (span_len - 1)]  137 us
    all_to_all x1, blocking collectives, on_device(): lax.all_to_all(grad_up_rows, 'seq', split_axis=1, concat_axis=0, tiled=True)  85.9 us
    all_to_all x1, waiting for transfers between devices, on_device(): lax.all_to_all(hidden, 'seq', split_axis=1, concat_axis=0, tiled=True)  77.7 us
    another operation x3, loops' own time, over_blocks(): state, unused = lax.scan(block_fn, state, scan_items)  57.9 us
    slice x8, local copies, waits for them, and re-layouts, bias_block(): repeated.reshape(lookup.shape[1], row_count, span_len - 1)[:, :, :col_count]  54.5 us
    dot_general x8, matrix products, masked_scores(): jnp.einsum('sqhe,skhe->shqk', query_four, keys_four, preferred_element_ty...  50.6 us
  transfers between devices with their start and end apart: 30, of which 11 were waited for; matrix products, arithmetic and copies ran while one was open for 69% of the time, Pallas kernels for 0%

commit v1 on v0

v1 whole, which is shorter than its diff:
```python
import math
from functools import partial

import jax
import jax.numpy as jnp
import numpy as np
from jax import lax
from jax.experimental import pallas as pl
from jax.experimental.pallas import tpu as pltpu
from jax.sharding import PartitionSpec as P

HEADS = 6
BUCKETS = 32
MAX_DOC = 800
BLK = 256
SPAN = 1024
EPS = 1e-06
MASKED = -1e30
F32 = jnp.float32
BF16 = jnp.bfloat16
VMEM_CAP = 58 * 1024 * 1024
GELU_K = math.sqrt(2.0 / math.pi)
GELU_A = 0.044715


def bucket_table():
    relative = np.arange(SPAN) - SPAN // 2
    distance = np.abs(relative)
    steps = np.array([12, 16, 23, 32, 46, 64, 91])
    levels = (distance[:, None] >= steps[None, :]).sum(axis=1)
    inside = np.where(distance < 8, distance, 8 + levels)
    return (inside + 16 * (relative > 0)).astype(np.int32)


class Moves:
    def __init__(self, n_dp, n_seq):
        self.n_dp, self.n_seq = n_dp, n_seq
        plane = n_dp // 2
        side = int(round(math.sqrt(plane)))
        self.size = {"a": plane // side, "b": side, "c": 2, "z": n_seq}
        dp = lax.axis_index("dp")
        self.index = {
            "a": dp // (2 * side),
            "b": (dp // 2) % side,
            "c": dp % 2,
            "z": lax.axis_index("seq"),
        }

    def rotate(self, x, axis):
        n = self.size[axis]
        if axis == "z":
            return lax.ppermute(x, "seq", [(i, (i + 1) % n) for i in range(n)])
        pairs = []
        side = self.size["b"]
        for i in range(self.n_dp):
            a, b, c = i // (2 * side), (i // 2) % side, i % 2
            if axis == "a":
                a = (a + 1) % n
            elif axis == "b":
                b = (b + 1) % n
            else:
                c = 1 - c
            pairs.append((i, (a * side + b) * 2 + c))
        return lax.ppermute(x, "dp", pairs)

    def zperm(self, x, pairs):
        return lax.ppermute(x, "seq", pairs)

    def gather(self, x, axis, at=0):
        n, i = self.size[axis], self.index[axis]
        if n == 2:
            other = self.rotate(x, axis)
            return ordered(i == 0, x, other, at)
        parts = [x]
        for _ in range(n - 1):
            parts.append(self.rotate(parts[-1], axis))
        turned = jnp.stack(parts[::-1] + parts[::-1], 0)
        full = lax.dynamic_slice_in_dim(turned, n - 1 - i, n, 0)
        return jnp.moveaxis(full, 0, at)

    def scatter(self, x, axis, at=0, out=BF16):
        n, i = self.size[axis], self.index[axis]
        take = lambda k: lax.dynamic_index_in_dim(x, k, at, keepdims=False)
        if n == 2:
            other = self.rotate(take(1 - i), axis)
            return add(take(i), other, out)
        acc = take((i + n - 1) % n)
        for step in range(n - 1):
            got = self.rotate(acc, axis)
            last = step == n - 2
            acc = add(take((i + 2 * n - 2 - step) % n), got, out if last else BF16)
        return acc


def add(x, y, out):
    return (x.astype(F32) + y.astype(F32)).astype(out)


def ordered(first, x, y, at):
    return jnp.stack([jnp.where(first, x, y), jnp.where(first, y, x)], at)


def z_pairs(mv, w):
    z = mv.index["z"]
    near = mv.zperm(w, [(0, 1), (1, 0), (2, 3), (3, 2)])
    pair = ordered(z % 2 == 0, w, near, 0)
    mid = mv.zperm(pair, [(1, 2), (2, 1)])
    far = mv.zperm(mid, [(1, 0), (2, 3)])
    got = jnp.where((z == 1) | (z == 2), mid, far)
    return pair, got


def z_gather(mv, w):
    if mv.n_seq != 4:
        return mv.gather(w, "z")
    pair, got = z_pairs(mv, w)
    low = mv.index["z"] < 2
    return ordered(low, pair, got, 0).reshape((4,) + w.shape)


def core_halves(mv, w):
    c = mv.index["c"]
    if mv.n_seq == 4:
        pair, got = z_pairs(mv, w)
        mine = (mv.index["z"] // 2) == c
        return jnp.where(mine, pair, got), jnp.where(mine, got, pair)
    full = mv.gather(w, "z")
    halves = full.reshape((2, mv.n_seq // 2) + w.shape)
    take = lambda k: lax.dynamic_index_in_dim(halves, k, 0, keepdims=False)
    return take(c), take(1 - c)


def gather_ffn(mv, w):
    c = mv.index["c"]
    k, rows, cols = w.shape
    keep, send = core_halves(mv, w)
    recv = mv.rotate(send, "c")
    block = ordered(c == 0, keep, recv, 2)
    zh = block.shape[0]
    result = []
    for j in range(zh):
        one = block[j].reshape(k, 2 * rows, cols)
        if j % 2 == 0:
            one = mv.gather(one, "b", 1)
            one = mv.gather(one, "a", 1)
        else:
            one = mv.gather(one, "a", 1)
            one = mv.gather(one, "b", 2)
        result.append(one.reshape(k, mv.n_dp * rows, cols))
    return result


def scatter_ffn_plane(mv, grad, j):
    k, depth, cols = grad.shape
    rows = depth // mv.n_dp
    na, nb = mv.size["a"], mv.size["b"]
    x = grad.reshape(k, na, nb, 2 * rows, cols)
    if j % 2 == 0:
        x = mv.scatter(x, "a", 1)
        x = mv.scatter(x, "b", 1)
    else:
        x = mv.scatter(x, "b", 2)
        x = mv.scatter(x, "a", 1)
    x = x.reshape(k, 2, rows, cols)
    c = mv.index["c"]
    take = lambda i: lax.dynamic_index_in_dim(x, i, 1, keepdims=False)
    keep = take(c)
    recv = mv.rotate(take(1 - c), "c")
    return ordered(c == 0, keep, recv, 0)


def scatter_ffn_z(mv, planes):
    z = mv.index["z"]
    if mv.n_seq != 4:
        full = jnp.stack(planes, 1)
        full = full.reshape((mv.n_seq,) + planes[0].shape[1:])
        return mv.scatter(full, "z", 0, F32)
    sums = []
    for j, x in enumerate(planes):
        take = lambda i: lax.dynamic_index_in_dim(x, i, 0, keepdims=False)
        high = z // 2
        recv = mv.zperm(take(1 - high), [(0, 2), (2, 0), (1, 3), (3, 1)])
        part = add(take(high), recv, BF16)
        recv = mv.zperm(part, [(1 - j, j), (3 - j, 2 + j)])
        sums.append(add(part, recv, F32))
    return jnp.where(z % 2 == 0, sums[0], sums[1])


def gather_small(mv, w):
    full = z_gather(mv, w)
    half = mv.n_seq // 2
    lo = mv.gather(mv.gather(full[:half], "b", 1), "a", 1)
    hi = mv.gather(mv.gather(full[half:], "a", 1), "b", 2)
    both = jnp.concatenate([lo, hi], 0)
    both = mv.gather(both, "c", 3)
    return both.reshape((mv.n_seq, mv.n_dp) + w.shape)


def scatter_small(mv, g):
    na, nb = mv.size["a"], mv.size["b"]
    zs, _, rp, cols = g.shape
    x = g.reshape(zs, na, nb, 2, rp, cols)
    x = mv.scatter(x, "c", 3)
    half = zs // 2
    lo = mv.scatter(mv.scatter(x[:half], "a", 1), "b", 1)
    hi = mv.scatter(mv.scatter(x[half:], "b", 2), "a", 1)
    x = jnp.concatenate([lo, hi], 0)
    if zs != 4:
        return mv.scatter(x, "z", 0, F32)
    z = mv.index["z"]
    x = x.reshape(2, 2, rp, cols)
    take = lambda i: lax.dynamic_index_in_dim(x, i, 0, keepdims=False)
    recv = mv.zperm(take(1 - z // 2), [(0, 2), (2, 0), (1, 3), (3, 1)])
    x = add(take(z // 2), recv, BF16)
    take = lambda i: lax.dynamic_index_in_dim(x, i, 0, keepdims=False)
    recv = mv.zperm(take(1 - z % 2), [(0, 1), (1, 0), (2, 3), (3, 2)])
    return add(take(z % 2), recv, F32)


def halo(mv, x, fill):
    rows = x.shape[0]
    n = mv.n_seq
    need = MAX_DOC
    left, right = [], []
    step = 1
    while need > 0 and step < n:
        take = min(rows, need)
        up = x if take == rows else x[rows - take :]
        down = x if take == rows else x[:take]
        left.insert(0, mv.zperm(up, [(i, i + step) for i in range(n - step)]))
        right.append(mv.zperm(down, [(i + step, i) for i in range(n - step)]))
        need -= take
        step += 1
    have = sum(part.shape[0] for part in left)
    pad = jnp.zeros((fill - have,) + x.shape[1:], x.dtype)
    return jnp.concatenate([pad] + left + [x] + right + [pad], 0)


def nt(x, y):
    return lax.dot_general(x, y, (((1,), (1,)), ((), ())), preferred_element_type=F32)


def nn(x, y):
    return lax.dot_general(x, y, (((1,), (0,)), ((), ())), preferred_element_type=F32)


def make_tiles(vec_ref, tiles):
    for h in range(HEADS):
        line = vec_ref[h : h + 1, :]
        wide = jnp.broadcast_to(line, (BLK, SPAN))
        rolled = pltpu.roll(wide, 0, 1, stride=1, stride_axis=0)
        tiles[h * 5] = jnp.broadcast_to(line[:, :1], (BLK, BLK))
        tiles[h * 5 + 4] = jnp.broadcast_to(line[:, SPAN - 1 :], (BLK, BLK))
        for d in (-1, 0, 1):
            at = SPAN // 2 + BLK * d
            tiles[h * 5 + 2 + d] = rolled[:, at : at + BLK]


def pair_masks(x):
    lane = lax.broadcasted_iota(jnp.int32, x.shape, 1)
    zero = jnp.zeros_like(x)
    return jnp.where(lane < 64, x, zero), jnp.where(lane < 64, zero, x)


def class_of(kb, own):
    return jnp.clip(kb - own, -2, 2) + 2


def forward_kernel(off, lohi, vec, q_ref, segq, kv, segk, out, exact, lse, tiles):
    i = pl.program_id(0)

    @pl.when(i == 0)
    def _():
        make_tiles(vec, tiles)

    own = off // BLK + i
    inner = HEADS * 64
    low, high = lohi[i, 0], lohi[i, 1]
    lane = lax.broadcasted_iota(jnp.int32, (BLK, 128), 1)
    seg_col = segq[...]
    for pair in range(HEADS // 2):
        cols = slice(pair * 128, pair * 128 + 128)
        vcols = slice(inner + pair * 128, inner + pair * 128 + 128)
        qs = pair_masks(q_ref[:, cols])

        def body(kb, state):
            rows = pl.ds(pl.multiple_of(kb * BLK, BLK), BLK)
            keys, values = kv[rows, cols], kv[rows, vcols]
            same = seg_col == segk[kb]
            kind = class_of(kb, own)
            new = []
            for e in range(2):
                peak, total, acc = state[e]
                s = nt(qs[e], keys) + tiles[(pair * 2 + e) * 5 + kind]
                s = jnp.where(same, s, MASKED)
                top = jnp.maximum(peak, jnp.max(s, axis=1, keepdims=True))
                fade = jnp.exp(peak - top)
                p = jnp.exp(s - top)
                total = total * fade + jnp.sum(p, axis=1, keepdims=True)
                acc = acc * fade + nn(p.astype(BF16), values)
                new.append((top, total, acc))
            return tuple(new)

        start = (
            jnp.full((BLK, 1), MASKED, F32),
            jnp.zeros((BLK, 1), F32),
            jnp.zeros((BLK, 128), F32),
        )
        state = lax.fori_loop(low, high, body, (start, start))
        done = []
        for e in range(2):
            peak, total, acc = state[e]
            done.append(acc / total)
            h = pair * 2 + e
            lse[:, h : h + 1] = peak + jnp.log(total)
        merged = jnp.where(lane < 64, done[0], done[1])
        out[:, cols] = merged.astype(BF16)
        exact[:, cols] = merged


def query_kernel(off, lohi, vec, q_ref, do_ref, stat, segq, kv, segk, dq, near, far, tiles, sums):
    i = pl.program_id(0)

    @pl.when(i == 0)
    def _():
        make_tiles(vec, tiles)
        sums[...] = jnp.zeros_like(sums)

    own = off // BLK + i
    inner = HEADS * 64
    low, high = lohi[i, 0], lohi[i, 1]
    lane = lax.broadcasted_iota(jnp.int32, (BLK, 128), 1)
    seg_col = segq[...]
    for pair in range(HEADS // 2):
        cols = slice(pair * 128, pair * 128 + 128)
        vcols = slice(inner + pair * 128, inner + pair * 128 + 128)
        qs = pair_masks(q_ref[:, cols])
        dos = pair_masks(do_ref[:, cols])

        def body(kb, state):
            rows = pl.ds(pl.multiple_of(kb * BLK, BLK), BLK)
            keys, values = kv[rows, cols], kv[rows, vcols]
            same = seg_col == segk[kb]
            kind = class_of(kb, own)
            new = []
            for e in range(2):
                h = pair * 2 + e
                s = nt(qs[e], keys) + tiles[h * 5 + kind]
                s = jnp.where(same, s, MASKED)
                p = jnp.exp(s - stat[:, h : h + 1])
                dp = nt(dos[e], values)
                ds = p * (dp - stat[:, 8 + h : 9 + h])
                at = h * 5 + kind
                sums[at] = sums[at] + ds
                new.append(state[e] + nn(ds.astype(BF16), keys))
            return tuple(new)

        start = jnp.zeros((BLK, 128), F32)
        state = lax.fori_loop(low, high, body, (start, start))
        dq[:, cols] = jnp.where(lane < 64, state[0], state[1]).astype(BF16)

    @pl.when(i == pl.num_programs(0) - 1)
    def _():
        for h in range(HEADS):
            zero = jnp.zeros((BLK, BLK), F32)
            x = jnp.concatenate([sums[h * 5 + 1], sums[h * 5 + 2], sums[h * 5 + 3], zero], axis=1)
            n = BLK // 2
            while n >= 8:
                x = x[:n] + pltpu.roll(x[n:], SPAN - n, 1)
                n //= 2
            row = lax.broadcasted_iota(jnp.int32, x.shape, 0)
            for n in (4, 2, 1):
                x = jnp.where((row & n) != 0, pltpu.roll(x, SPAN - n, 1), x)
            near[h] = x
            far[h, 0] = jnp.sum(sums[h * 5].reshape(BLK // 8, 8, BLK), axis=0)
            far[h, 1] = jnp.sum(sums[h * 5 + 4].reshape(BLK // 8, 8, BLK), axis=0)


def key_kernel(off, lohi, vec, kv_ref, segk, qd, stat, segq, dkv, tiles):
    i = pl.program_id(0)

    @pl.when(i == 0)
    def _():
        make_tiles(vec, tiles)

    own = off // BLK + i
    inner = HEADS * 64
    low, high = lohi[i, 0], lohi[i, 1]
    lane = lax.broadcasted_iota(jnp.int32, (BLK, 128), 1)
    seg_col = segk[...]
    for pair in range(HEADS // 2):
        cols = slice(pair * 128, pair * 128 + 128)
        vcols = slice(inner + pair * 128, inner + pair * 128 + 128)
        ks = pair_masks(kv_ref[:, cols])
        vs = pair_masks(kv_ref[:, vcols])

        def body(qb, state):
            rows = pl.ds(pl.multiple_of(qb * BLK, BLK), BLK)
            queries, answers = qd[rows, cols], qd[rows, vcols]
            same = seg_col == segq[qb]
            kind = class_of(qb, own)
            new = []
            for e in range(2):
                h = pair * 2 + e
                s = nt(ks[e], queries) + tiles[h * 5 + kind]
                s = jnp.where(same, s, MASKED)
                p = jnp.exp(s - stat[qb, h : h + 1, :])
                dp = nt(vs[e], answers)
                ds = p * (dp - stat[qb, 8 + h : 9 + h, :])
                dk, dv = state[e]
                dk = dk + nn(ds.astype(BF16), queries)
                dv = dv + nn(p.astype(BF16), answers)
                new.append((dk, dv))
            return tuple(new)

        start = jnp.zeros((BLK, 128), F32)
        state = lax.fori_loop(low, high, body, ((start, start), (start, start)))
        dkv[:, cols] = jnp.where(lane < 64, state[0][0], state[1][0]).astype(BF16)
        dkv[:, vcols] = jnp.where(lane < 64, state[0][1], state[1][1]).astype(BF16)


def whole_block(shape):
    return pl.BlockSpec(shape, lambda i: (0,) * len(shape))


def row_block(cols):
    return pl.BlockSpec((BLK, cols), lambda i: (i, 0))


SMEM_SPEC = pl.BlockSpec(memory_space=pltpu.SMEM)
ATTN_PARAMS = dict(
    compiler_params=pltpu.CompilerParams(
        dimension_semantics=("arbitrary",), vmem_limit_bytes=VMEM_CAP
    )
)
TILES = pltpu.VMEM((HEADS * 5, BLK, BLK), F32)


def attend(off, lohi, vec, q, seg_col, kv, seg_row):
    rows, inner = q.shape
    return pl.pallas_call(
        partial(forward_kernel, off),
        grid=(rows // BLK,),
        in_specs=[
            SMEM_SPEC,
            whole_block(vec.shape),
            row_block(inner),
            row_block(1),
            whole_block(kv.shape),
            whole_block(seg_row.shape),
        ],
        out_specs=[row_block(inner), row_block(inner), row_block(128)],
        out_shape=[
            jax.ShapeDtypeStruct((rows, inner), BF16),
            jax.ShapeDtypeStruct((rows, inner), F32),
            jax.ShapeDtypeStruct((rows, 128), F32),
        ],
        scratch_shapes=[TILES],
        cost_estimate=pl.CostEstimate(
            flops=rows * 1280 * inner * 4 * 4, bytes_accessed=8 * 2**20, transcendentals=0
        ),
        name="attend",
        **ATTN_PARAMS,
    )(lohi, vec, q, seg_col, kv, seg_row)


def attend_queries(off, lohi, vec, q, do, stat, seg_col, kv, seg_row):
    rows, inner = q.shape
    return pl.pallas_call(
        partial(query_kernel, off),
        grid=(rows // BLK,),
        in_specs=[
            SMEM_SPEC,
            whole_block(vec.shape),
            row_block(inner),
            row_block(inner),
            row_block(128),
            row_block(1),
            whole_block(kv.shape),
            whole_block(seg_row.shape),
        ],
        out_specs=[
            row_block(inner),
            whole_block((HEADS, 8, SPAN)),
            whole_block((HEADS, 2, 8, BLK)),
        ],
        out_shape=[
            jax.ShapeDtypeStruct((rows, inner), BF16),
            jax.ShapeDtypeStruct((HEADS, 8, SPAN), F32),
            jax.ShapeDtypeStruct((HEADS, 2, 8, BLK), F32),
        ],
        scratch_shapes=[TILES, TILES],
        cost_estimate=pl.CostEstimate(
            flops=rows * 1280 * inner * 6 * 4, bytes_accessed=8 * 2**20, transcendentals=0
        ),
        name="attend_queries",
        **ATTN_PARAMS,
    )(lohi, vec, q, do, stat, seg_col, kv, seg_row)


def attend_keys(off, lohi, vec, kv, seg_col, qd, stat, seg_row):
    rows, wide = kv.shape
    return pl.pallas_call(
        partial(key_kernel, off),
        grid=(rows // BLK,),
        in_specs=[
            SMEM_SPEC,
            whole_block(vec.shape),
            row_block(wide),
            row_block(1),
            whole_block(qd.shape),
            whole_block(stat.shape),
            whole_block(seg_row.shape),
        ],
        out_specs=row_block(wide),
        out_shape=jax.ShapeDtypeStruct((rows, wide), BF16),
        scratch_shapes=[TILES],
        cost_estimate=pl.CostEstimate(
            flops=rows * 1280 * wide * 4 * 4, bytes_accessed=8 * 2**20, transcendentals=0
        ),
        name="attend_keys",
        **ATTN_PARAMS,
    )(lohi, vec, kv, seg_col, qd, stat, seg_row)


def ffn_kernel(nm, n2, ct, n2t, ctt, wg, wu, wd, out, gn2, dw, hid, ggr, gur):
    i = pl.program_id(0)

    @pl.when(i < nm)
    def _():
        rows = pl.ds(pl.multiple_of(i * BLK, BLK), BLK)
        x = n2[...]
        g = nn(x, wg[...])
        u = nn(x, wu[...])
        gh = nn(ct[...], wd[...])
        square = g * g
        t = jnp.tanh(GELU_K * g * (1.0 + GELU_A * square))
        half = 0.5 * (1.0 + t)
        gelu = g * half
        slope = half + 0.5 * g * (1.0 - t * t) * (GELU_K * (1.0 + 3.0 * GELU_A * square))
        h = (gelu * u).astype(BF16)
        gg = (gh * u * slope).astype(BF16)
        gu = (gh * gelu).astype(BF16)
        hid[rows, :] = h
        ggr[rows, :] = gg
        gur[rows, :] = gu
        out[...] = nt(h, wd[...]).astype(BF16)
        gn2[...] = (nt(gg, wg[...]) + nt(gu, wu[...])).astype(BF16)

    @pl.when(i >= nm)
    def _():
        x = n2t[...]
        dw[0] = nn(x, ggr[...]).astype(BF16)
        dw[1] = nn(x, gur[...]).astype(BF16)
        dw[2] = nn(ctt[...], hid[...]).astype(BF16)


def ffn(n2, ct, n2t, ctt, wg, wu, wd):
    m, depth = n2.shape
    cols = wg.shape[1]
    nm = m // BLK
    nr = 4
    tile = depth // nr
    first = lambda i: (jnp.minimum(i, nm - 1), 0)
    later = lambda i: (jnp.maximum(i - nm, 0), 0)
    weight = pl.BlockSpec((depth, cols), lambda i: (0, 0), pipeline_mode=pl.Buffered(1))
    return pl.pallas_call(
        partial(ffn_kernel, nm),
        grid=(nm + nr,),
        in_specs=[
            pl.BlockSpec((BLK, depth), first),
            pl.BlockSpec((BLK, depth), first),
            pl.BlockSpec((tile, m), later),
            pl.BlockSpec((tile, m), later),
            weight,
            weight,
            weight,
        ],
        out_specs=[
            pl.BlockSpec((BLK, depth), first),
            pl.BlockSpec((BLK, depth), first),
            pl.BlockSpec((3, tile, cols), lambda i: (0, jnp.maximum(i - nm, 0), 0)),
        ],
        out_shape=[
            jax.ShapeDtypeStruct((m, depth), BF16),
            jax.ShapeDtypeStruct((m, depth), BF16),
            jax.ShapeDtypeStruct((3, depth, cols), BF16),
        ],
        scratch_shapes=[pltpu.VMEM((m, cols), BF16)] * 3,
        cost_estimate=pl.CostEstimate(
            flops=18 * m * depth * cols, bytes_accessed=32 * 2**20, transcendentals=0
        ),
        name="ffn",
        compiler_params=pltpu.CompilerParams(
            dimension_semantics=("arbitrary",), vmem_limit_bytes=VMEM_CAP
        ),
    )(n2, ct, n2t, ctt, wg, wu, wd)


def rms_scale(x):
    return lax.rsqrt(jnp.mean(x * x, axis=-1, keepdims=True) + EPS)


def norm_back(grad, x, scale, gain):
    gain_grad = jnp.sum(grad * (x * scale), axis=0)
    weighted = grad * gain
    dots = jnp.mean(weighted * x, axis=-1, keepdims=True)
    return scale * weighted - x * (scale * scale * scale * dots), gain_grad


def split_heads_z(x, n_seq):
    rows, inner = x.shape
    return jnp.transpose(x.reshape(rows, n_seq, inner // n_seq), (1, 0, 2))


def on_device(
    n_dp,
    n_seq,
    inputs,
    segments,
    cotangent,
    w_query,
    w_key,
    w_value,
    w_out,
    w_gate,
    w_up,
    w_down,
    gain_attn,
    gain_ffn,
    rel_table,
):
    mv = Moves(n_dp, n_seq)
    seqs, rows, depth = inputs.shape
    source = inputs.reshape(seqs * rows, depth).astype(F32)
    tangent = cotangent.reshape(seqs * rows, depth)
    rw = w_query.shape[0]
    sc = w_query.shape[1]
    inner = sc * n_seq
    rp = -(-(rw + 2) // 16) * 16

    body = jnp.concatenate([w_query, w_key, w_value, w_out.T], axis=1)
    gains = jnp.concatenate([gain_attn, gain_ffn])
    table_row = rel_table.reshape(-1)
    pad_to = lambda v: jnp.pad(v, (0, 4 * sc - v.shape[0]))[None]
    packed = jnp.concatenate(
        [body, pad_to(gains), pad_to(table_row), jnp.zeros((rp - rw - 2, 4 * sc), BF16)], axis=0
    )
    att = gather_small(mv, packed)
    full = att[:, :, :rw, :].reshape(n_seq, depth, 4 * sc)
    gain_one = att[0, :, rw, :rw].reshape(depth).astype(F32)
    gain_two = att[0, :, rw, rw : 2 * rw].reshape(depth).astype(F32)
    table = att[0, :, rw + 1, : table_row.shape[0]].reshape(BUCKETS, HEADS)

    weights_down = gather_ffn(mv, w_down.T[None])
    weights_pair = gather_ffn(mv, jnp.stack([w_gate, w_up]))

    scale_one = rms_scale(source)
    normed = ((source * scale_one) * gain_one).astype(BF16)
    qkv = jnp.einsum("td,zdc->ztc", normed, full[:, :, : 3 * sc], preferred_element_type=F32)
    qkv = jnp.transpose(qkv.astype(BF16).reshape(n_seq, rows, 3, sc), (1, 2, 0, 3))
    qkv = qkv.reshape(rows, 3 * inner)
    q = qkv[:, :inner]
    kv = qkv[:, inner:]

    off = -(-MAX_DOC // BLK) * BLK
    blocks = (2 * off + rows) // BLK
    seg_own = segments.reshape(rows)
    seg_all = halo(mv, (seg_own + 1).reshape(rows, 1), off)[:, 0] - 1
    seg_row = seg_all.reshape(blocks, 1, BLK)
    seg_col = seg_own.reshape(rows, 1)
    spots = jnp.arange(seg_all.shape[0], dtype=jnp.int32)
    firsts = seg_own[::BLK]
    lasts = seg_own[BLK - 1 :: BLK]
    low = jnp.min(jnp.where(seg_all[None] == firsts[:, None], spots[None], 1 << 20), axis=1) // BLK
    high = jnp.max(jnp.where(seg_all[None] == lasts[:, None], spots[None], -1), axis=1) // BLK + 1
    lohi = jnp.stack([low, high], 1).astype(jnp.int32)

    buckets = bucket_table()
    chosen = jnp.asarray((buckets[:, None] == np.arange(BUCKETS)[None, :]), BF16)
    vec = lax.dot_general(
        table, chosen, (((0,), (1,)), ((), ())), preferred_element_type=F32
    )
    vec_back = jnp.roll(vec[:, ::-1], 1, axis=1)
    vec_back = vec_back.at[:, 0].set(vec[:, SPAN - 1])

    kv_all = halo(mv, kv, off)
    attended, exact, lse = attend(off, lohi, vec, q, seg_col, kv_all, seg_row)
    q_all = halo(mv, q, off)

    mixed = source + jnp.einsum(
        "tzc,zdc->td",
        attended.reshape(rows, n_seq, sc),
        full[:, :, 3 * sc :],
        preferred_element_type=F32,
    )
    scale_two = rms_scale(mixed)
    normed_two = ((mixed * scale_two) * gain_two).astype(BF16)

    n2 = jnp.concatenate([normed_two, mv.rotate(normed_two, "c")], 0)
    ct = jnp.concatenate([tangent, mv.rotate(tangent, "c")], 0)
    n2t, ctt = n2.T, ct.T
    outs, gn2s, planes = [], [], []
    for j in range(n_seq // 2):
        out_part, gn2_part, dw = ffn(
            n2, ct, n2t, ctt, weights_pair[j][0], weights_pair[j][1], weights_down[j][0]
        )
        outs.append(out_part.astype(F32))
        gn2s.append(gn2_part.astype(F32))
        planes.append(scatter_ffn_plane(mv, dw, j))
    gn2 = sum(gn2s)
    grad_n2 = gn2[:rows] + mv.rotate(gn2[rows:].astype(BF16), "c").astype(F32)
    out_sum = sum(outs)
    outputs = mixed + out_sum[:rows] + mv.rotate(out_sum[rows:].astype(BF16), "c").astype(F32)
    outputs = outputs.astype(BF16)
    own_ffn = scatter_ffn_z(mv, planes)

    grad_mixed, grad_gain_two = norm_back(grad_n2, mixed, scale_two, gain_two)
    grad_mixed = grad_mixed + tangent.astype(F32)
    grad_branch = grad_mixed.astype(BF16)
    grad_att = jnp.einsum(
        "td,zdc->tzc", grad_branch, full[:, :, 3 * sc :], preferred_element_type=F32
    )
    grad_att = grad_att.reshape(rows, inner).astype(BF16)
    delta = jnp.sum(
        (grad_att.astype(F32) * exact).reshape(rows, HEADS, inner // HEADS), axis=2
    )
    stat = jnp.concatenate([lse[:, :8], jnp.pad(delta, ((0, 0), (0, 120)))], axis=1)
    stat_all = halo(mv, stat[:, :16], off)
    stat_rows = jnp.transpose(stat_all.reshape(blocks, BLK, 16), (0, 2, 1))
    qd_all = jnp.concatenate([q_all, halo(mv, grad_att, off)], axis=1)

    dq, near, far = attend_queries(off, lohi, vec, q, grad_att, stat, seg_col, kv_all, seg_row)
    dkv = attend_keys(off, lohi, vec_back, kv, seg_col, qd_all, stat_rows, seg_row)

    sheared = jnp.sum(near, axis=1)
    sheared = jnp.roll(sheared, BLK, axis=1)
    grad_table = jnp.dot(
        sheared, chosen.astype(F32), precision=lax.Precision.HIGHEST
    ).T
    far_sums = jnp.sum(far, axis=(2, 3))
    grad_table = grad_table.at[15].add(far_sums[:, 0]).at[31].add(far_sums[:, 1])

    rows_z = jnp.concatenate(
        [split_heads_z(dq, n_seq), split_heads_z(dkv[:, :inner], n_seq), split_heads_z(dkv[:, inner:], n_seq)],
        axis=2,
    )
    grad_normed = jnp.einsum(
        "ztc,zdc->td", rows_z, full[:, :, : 3 * sc], preferred_element_type=F32
    )
    grad_source, grad_gain_one = norm_back(grad_normed, source, scale_one, gain_one)
    input_grad = (grad_mixed + grad_source).astype(BF16)

    g_in = jnp.einsum("td,ztc->zdc", normed, rows_z, preferred_element_type=F32)
    g_out = jnp.einsum(
        "td,ztc->zdc", grad_branch, split_heads_z(attended, n_seq), preferred_element_type=F32
    )
    grads = jnp.concatenate([g_in, g_out], axis=2).reshape(n_seq, n_dp, rw, 4 * sc)
    gain_rows = jnp.concatenate(
        [grad_gain_one.reshape(n_dp, rw), grad_gain_two.reshape(n_dp, rw)], axis=1
    )
    widen = lambda v: jnp.broadcast_to(
        jnp.pad(v, ((0, 0), (0, 4 * sc - v.shape[1])))[None, :, None, :], (n_seq, n_dp, 1, 4 * sc)
    )
    table_rows = grad_table.reshape(n_dp, -1)
    grads = jnp.concatenate(
        [
            grads,
            widen(gain_rows),
            widen(table_rows),
            jnp.zeros((n_seq, n_dp, rp - rw - 2, 4 * sc), F32),
        ],
        axis=2,
    ).astype(BF16)
    own = scatter_small(mv, grads)

    return (
        outputs.reshape(seqs, rows, depth),
        input_grad.reshape(seqs, rows, depth),
        own[:rw, :sc],
        own[:rw, sc : 2 * sc],
        own[:rw, 2 * sc : 3 * sc],
        own[:rw, 3 * sc :].T,
        own_ffn[0],
        own_ffn[1],
        own_ffn[2].T,
        own[rw, :rw],
        own[rw, rw : 2 * rw],
        own[rw + 1, : table_row.shape[0]].reshape(rel_table.shape),
    )


def solution(mesh):
    row, col = P("dp", "seq"), P("seq", "dp")
    tokens = P("dp", "seq", None)
    return jax.shard_map(
        partial(on_device, mesh.shape["dp"], mesh.shape["seq"]),
        mesh=mesh,
        in_specs=(tokens, row, tokens, row, row, row, col, row, row, col, P("dp"), P("dp"), P("dp", None)),
        out_specs=(tokens, tokens, row, row, row, col, row, row, col, P("dp"), P("dp"), P("dp", None)),
        check_vma=False,
    )
```

time: 2200 us -> 834 us (0.38)
  local copies, waits for them, and re-layouts: 1160 us -> 140 us
  blocking collectives: 246 us -> 0 us
  matrix products: 263 us -> 26.2 us
  Pallas kernels: 0 us -> 132 us
  starting transfers between devices: 30.7 us -> 137 us
  loops' own time: 57.9 us -> 0 us
  waiting for transfers between devices: 300 us -> 252 us
  other arithmetic: 102 us -> 135 us
    while x81 -> x0, local copies, waits for them, and re-layouts: 588 us -> none
    ppermute x0 -> x65, waiting for transfers between devices: none -> 252 us  [the longest x35 174 us: zperm(): return lax.ppermute(x, 'seq', pairs)]
    dot_general x69 -> x8, matrix products: 263 us -> 25.4 us  [the longest x1 7.15 us: on_device(): jnp.einsum('ztc,zdc->td', rows_z, full[:, :, :3 * sc], preferred_element_...]
    reshape x16 -> x7, local copies, waits for them, and re-layouts: 226 us -> 2.64 us  [the longest x1 0.84 us: on_device(): seg_own = segments.reshape(rows)]
    slice x21 -> x28, local copies, waits for them, and re-layouts: 194 us -> 24.6 us  [the longest x7 4.55 us: halo(): down = x if take == rows else x[:take]]
    all_gather x18 -> x0, waiting for transfers between devices: 160 us -> none  [the longest x1 35.3 us: on_device(): lax.all_gather(key_shard, 'seq', axis=1, tiled=True)]
    ppermute x0 -> x65, starting transfers between devices: none -> 137 us  [the longest x35 103 us: zperm(): return lax.ppermute(x, 'seq', pairs)]
    pallas_call x0 -> x5, Pallas kernels: none -> 132 us  [the longest x2 76 us: ffn(): pl.pallas_call(partial(ffn_kernel, nm), grid=(nm + nr,), in_specs=[pl.Blo...]
  transfers between devices with their start and end apart: 30 -> 65, of which waited for: 11 -> 21; matrix products, arithmetic and copies ran while one was open for 69% -> 33% of each run, Pallas kernels for 0% -> 14%
where the time goes in v1:
time: 834 us; the launch traced here: 824 us
  waiting for transfers between devices  252 us (30%)
  local copies, waits for them, and re-layouts  140 us (17%)
  starting transfers between devices  137 us (16%)
  other arithmetic  135 us (16%)
  Pallas kernels  132 us (16%)
  matrix products  26.2 us (3%)
    ppermute x35, waiting for transfers between devices, zperm(): return lax.ppermute(x, 'seq', pairs)  174 us
    ppermute x35, starting transfers between devices, zperm(): return lax.ppermute(x, 'seq', pairs)  103 us
    ppermute x30, waiting for transfers between devices, rotate(): return lax.ppermute(x, 'dp', pairs)  78.2 us
    pallas_call x2, Pallas kernels, ffn(): pl.pallas_call(partial(ffn_kernel, nm), grid=(nm + nr,), in_specs=[pl.Blo...  76 us
    unnamed x186, local copies, waits for them, and re-layouts  46.3 us
    another operation x37, other arithmetic, ordered(): return jnp.stack([jnp.where(first, x, y), jnp.where(first, y, x)], at)  44.1 us
    ppermute x30, starting transfers between devices, rotate(): return lax.ppermute(x, 'dp', pairs)  33.4 us
    convert_element_type x12, other arithmetic, add(): return (x.astype(F32) + y.astype(F32)).astype(out)  25.6 us
  transfers between devices with their start and end apart: 65, of which 21 were waited for; matrix products, arithmetic and copies ran while one was open for 33% of the time, Pallas kernels for 14%

profile of v1, /device:TPU:10, one launch (start us, length us, event | category | flops | bytes accessed | tf_op | source)
XLA Modules:
  0.0 824.0 jit_solution(10354416051727336635)
XLA Ops:
  12.9 4.6 collective-permute-start
  40.6 11.3 %collective-permute-done.6 = bf16[2,192,384]{2,1,0:T(8,128)(2,1)S(1)} collective-permute-done((bf16[2,192,384]{2,1,0:T(8,128)(2,1)}, bf16[2,192,384]{2,1,0:T(8,128)(2,1)S(1)}, u32[]{:S(2)}, u32[]{:S(2)}) %collective-permute-start.6) | collective-permute-done | bytes 294944 | tf_op jit(solution)/shard_map/ppermute | solution.py:67
  80.7 13.1 %collective-permute-done.19 = bf16[2,2,184,896]{3,2,1,0:T(8,128)(2,1)} collective-permute-done((bf16[2,2,184,896]{3,2,1,0:T(8,128)(2,1)S(1)}, bf16[2,2,184,896]{3,2,1,0:T(8,128)(2,1)}, u32[]{:S(2)}, u32[]{:S(2)}) %collective-permute-start.19) | collective-permute-done | bytes 1318944 | tf_op jit(solution)/shard_map/ppermute | solution.py:67
  129.3 4.8 fusion.29
  137.3 5.1 collective-permute-start.12
  155.4 5.8 collective-permute-done.12
  169.7 8.3 %collective-permute-done.13 = bf16[512,768]{1,0:T(8,128)(2,1)} collective-permute-done((bf16[512,768]{1,0:T(8,128)(2,1)S(1)}, bf16[512,768]{1,0:T(8,128)(2,1)}, u32[]{:S(2)}, u32[]{:S(2)}) %collective-permute-start.13) | collective-permute-done | bytes 786464 | tf_op jit(solution)/shard_map/ppermute | solution.py:67
  185.1 8.1 collective-permute-done.15
  196.8 20.5 %attend.1 = (bf16[512,384]{1,0:T(8,128)(2,1)}, f32[512,384]{1,0:T(8,128)}, f32[512,128]{1,0:T(8,128)}) custom-call(s32[2,2]{1,0:T(2,128)} %pad_add_fusion.lohi, f32[6,1024]{1,0:T(8,128)} %fusion.91.vec, bf16[512,384]{1,0:T(8,128)(2,1)} %copy.289.q_ref, s32[512,1]{1,0:T(8,128)} %copy.231.segq.segk, bf16[2560,768]{1,0:T(8,128)(2,1)} %broadcast_dynamic-update-slice_fusion.1.kv, ...), custom_call_target="tpu_custom_call" | custom-call | flops 4026531840 | bytes 8388608 | tf_op jit(solution)/shard_map/attend/pallas_call | solution.py:441
  227.6 9.7 %collective-permute-start.31 = (bf16[2,2,368,896]{3,2,0,1:T(8,128)(2,1)}, bf16[2,2,368,896]{3,2,0,1:T(8,128)(2,1)}, u32[]{:S(2)}, u32[]{:S(2)}) collective-permute-start(bf16[2,2,368,896]{3,2,0,1:T(8,128)(2,1)} %pad_maximum_fusion.9), channel_id=1, source_target_pairs={{0,8},{4,12},{8,0},{12,4},{16,24},{20,28},{24,16},{28,20},{1,9},{5... | collective-permute-start | bytes 7913480 | tf_op jit(solution)/shard_map/ppermute | solution.py:64
  253.7 12.4 %collective-permute-start.37 = (bf16[512,384]{1,0:T(8,128)(2,1)S(1)}, bf16[512,384]{1,0:T(8,128)(2,1)S(1)}, u32[]{:S(2)}, u32[]{:S(2)}) collective-permute-start(bf16[512,384]{1,0:T(8,128)(2,1)S(1)} %copy-done.51), channel_id=1, source_target_pairs={{0,1},{1,2},{2,3},{4,5},{5,6},{6,7},{8,9},{9,10},{10,11},{12,13},{... | collective-permute-start | bytes 1179656 | tf_op jit(solution)/shard_map/ppermute | solution.py:67
  277.4 5.2 fusion.82
  287.3 6.2 collective-permute-done.31
  308.1 37.7 %ffn.2 = (bf16[1024,1472]{1,0:T(8,128)(2,1)}, bf16[1024,1472]{1,0:T(8,128)(2,1)}, bf16[3,1472,896]{2,1,0:T(8,128)(2,1)}) custom-call(bf16[1024,1472]{1,0:T(8,128)(2,1)} %copy.243.n2, bf16[1024,1472]{1,0:T(8,128)(2,1)} %copy.244.ct, bf16[1472,1024]{1,0:T(8,128)(2,1)} %get-tuple-element.100.n2t, bf16[1472,1024]{1,0:T(8,128)(2,1)} %get-tuple-element.98.ctt, ...), custom_call_target="tpu_custom_call" | custom-call | flops 24310185984 | bytes 33554432 | tf_op jit(solution)/shard_map/ffn/pallas_call | solution.py:567
  345.8 4.7 copy.245
  350.5 38.2 %ffn.3 = (bf16[1024,1472]{1,0:T(8,128)(2,1)}, bf16[1024,1472]{1,0:T(8,128)(2,1)}, bf16[3,1472,896]{2,1,0:T(8,128)(2,1)}) custom-call(bf16[1024,1472]{1,0:T(8,128)(2,1)} %copy.243.n2, bf16[1024,1472]{1,0:T(8,128)(2,1)} %copy.244.ct, bf16[1472,1024]{1,0:T(8,128)(2,1)} %get-tuple-element.100.n2t, bf16[1472,1024]{1,0:T(8,128)(2,1)} %get-tuple-element.98.ctt, ...), custom_call_target="tpu_custom_call" | custom-call | flops 24310185984 | bytes 33554432 | tf_op jit(solution)/shard_map/ffn/pallas_call | solution.py:567
  388.7 4.7 copy.251
  393.4 4.7 copy.252
  398.2 4.7 copy.253
  438.3 18.1 %attend_queries.1 = (bf16[512,384]{1,0:T(8,128)(2,1)}, f32[6,8,1024]{2,1,0:T(8,128)}, f32[6,2,8,256]{3,2,1,0:T(8,128)}) custom-call(s32[2,2]{1,0:T(2,128)} %pad_add_fusion.lohi, f32[6,1024]{1,0:T(8,128)} %fusion.91.vec, bf16[512,384]{1,0:T(8,128)(2,1)} %copy.289.q_ref, bf16[512,384]{1,0:T(8,128)(2,1)} %copy.257.do_ref, f32[512,134]{1,0:T(8,128)} %select_maximum_fusion.stat, ...), custom_call_target="tpu_custom_call" | custom-call | flops 6039797760 | bytes 8388608 | tf_op jit(solution)/shard_map/attend_queries/pallas_call | solution.py:469
  458.7 17.5 %collective-permute-start.41 = (bf16[512,384]{1,0:T(8,128)(2,1)}, bf16[512,384]{1,0:T(8,128)(2,1)}, u32[]{:S(2)}, u32[]{:S(2)}) collective-permute-start(bf16[512,384]{1,0:T(8,128)(2,1)} %copy.257.do_ref), channel_id=1, source_target_pairs={{0,1},{1,2},{2,3},{4,5},{5,6},{6,7},{8,9},{9,10},{10,11},{12,13},{... | collective-permute-start | bytes 1179656 | tf_op jit(solution)/shard_map/ppermute | solution.py:67
  483.2 6.1 collective-permute-start.40
  497.4 5.3 collective-permute-done.44
  534.1 17.2 %attend_keys.1 = bf16[512,768]{1,0:T(8,128)(2,1)} custom-call(s32[2,2]{1,0:T(2,128)} %pad_add_fusion.lohi, f32[6,1024]{1,0:T(8,128)} %copy-done.66, bf16[512,768]{1,0:T(8,128)(2,1)} %copy-done.47, s32[512,1]{1,0:T(8,128)} %copy.231.segq.segk, bf16[2560,768]{1,0:T(8,128)(2,1)} %pad_maximum_fusion.2.qd, f32[10,16,256]{2,1,0:T(8,128)} %bitcast.398, ...), custom_call_target="tpu_custom_call" | custom-call | flops 8053063680 | bytes 8388608 | tf_op jit(solution)/shard_map/attend_keys/pallas_call | solution.py:503
  562.7 6.8 copy.278
  569.5 7.2 fusion.16
  584.7 15.1 %collective-permute-done.55 = bf16[3,2,368,896]{3,2,1,0:T(8,128)(2,1)} collective-permute-done((bf16[3,2,368,896]{3,2,1,0:T(8,128)(2,1)}, bf16[3,2,368,896]{3,2,1,0:T(8,128)(2,1)}, u32[]{:S(2)}, u32[]{:S(2)}) %collective-permute-start.55) | collective-permute-done | bytes 3956768 | tf_op jit(solution)/shard_map/ppermute | solution.py:64
  607.4 4.9 fusion
  621.9 47.9 %collective-permute-done.49 = bf16[2,2,192,384]{3,2,1,0:T(8,128)(2,1)} collective-permute-done((bf16[2,2,192,384]{3,2,1,0:T(8,128)(2,1)}, bf16[2,2,192,384]{3,2,1,0:T(8,128)(2,1)}, u32[]{:S(2)}, u32[]{:S(2)}) %collective-permute-start.49) | collective-permute-done | bytes 589856 | tf_op jit(solution)/shard_map/ppermute | solution.py:64
  691.9 90.4 %collective-permute-done.53 = bf16[2,192,384]{2,1,0:T(8,128)(2,1)S(1)} collective-permute-done((bf16[2,192,384]{2,1,0:T(8,128)(2,1)}, bf16[2,192,384]{2,1,0:T(8,128)(2,1)S(1)}, u32[]{:S(2)}, u32[]{:S(2)}) %collective-permute-start.53) | collective-permute-done | bytes 294944 | tf_op jit(solution)/shard_map/ppermute | solution.py:67
  799.7 12.3 %collective-permute-done.59 = bf16[3,184,896]{2,1,0:T(8,128)(2,1)} collective-permute-done((bf16[3,184,896]{2,1,0:T(8,128)(2,1)}, bf16[3,184,896]{2,1,0:T(8,128)(2,1)}, u32[]{:S(2)}, u32[]{:S(2)}) %collective-permute-start.59) | collective-permute-done | bytes 989216 | tf_op jit(solution)/shard_map/ppermute | solution.py:67
  812.0 7.7 collective-permute-done.64
  (489 shorter events, 355.0 us)
Async XLA Ops:
  1.5 32.3 %collective-permute-start.1 = (s32[512,1]{0,1:T(1,128)S(1)}, s32[512,1]{0,1:T(1,128)S(1)}, u32[]{:S(2)}, u32[]{:S(2)}) collective-permute-start(s32[512,1]{0,1:T(1,128)S(1)} %broadcast_add_fusion.1), channel_id=1, source_target_pairs={{0,1},{1,2},{2,3},{4,5},{5,6},{6,7},{8,9},{9,10},{10,11},{12,13},{... | collective-permute-start | bytes 6152 | tf_op jit(solution)/shard_map/ppermute | solution.py:67
  4.9 28.8 %collective-permute-start.2 = (s32[512,1]{0,1:T(1,128)S(1)}, s32[512,1]{0,1:T(1,128)S(1)}, u32[]{:S(2)}, u32[]{:S(2)}) collective-permute-start(s32[512,1]{0,1:T(1,128)S(1)} %broadcast_add_fusion.1), channel_id=1, source_target_pairs={{1,0},{2,1},{3,2},{5,4},{6,5},{7,6},{9,8},{10,9},{11,10},{13,12},{... | collective-permute-start | bytes 6152 | tf_op jit(solution)/shard_map/ppermute | solution.py:67
  7.3 26.6 %collective-permute-start.24 = (bf16[1,184,896]{2,1,0:T(8,128)(2,1)}, bf16[1,184,896]{2,1,0:T(8,128)(2,1)}, u32[]{:S(2)}, u32[]{:S(2)}) collective-permute-start(bf16[1,184,896]{2,1,0:T(8,128)(2,1)} %bitcast.394), channel_id=1, source_target_pairs={{0,1},{1,0},{2,3},{3,2},{4,5},{5,4},{6,7},{7,6},{8,9},{9,8},{10,11... | collective-permute-start | bytes 989192 | tf_op jit(solution)/shard_map/ppermute | solution.py:67
  33.8 63.6 %collective-permute-start.17 = (bf16[512,1472]{0,1:T(8,128)(2,1)S(1)}, bf16[512,1472]{0,1:T(8,128)(2,1)}, u32[]{:S(2)}, u32[]{:S(2)}) collective-permute-start(bf16[512,1472]{0,1:T(8,128)(2,1)S(1)} %bitcast.364), channel_id=1, source_target_pairs={{0,4},{4,0},{8,12},{12,8},{16,20},{20,16},{24,28},{28,24},{1,5},{5... | collective-permute-start | bytes 4521992 | tf_op jit(solution)/shard_map/ppermute | solution.py:64
  66.3 27.6 %collective-permute-start.19 = (bf16[2,2,184,896]{3,2,1,0:T(8,128)(2,1)S(1)}, bf16[2,2,184,896]{3,2,1,0:T(8,128)(2,1)}, u32[]{:S(2)}, u32[]{:S(2)}) collective-permute-start(bf16[2,2,184,896]{3,2,1,0:T(8,128)(2,1)S(1)} %pad_maximum_fusion.12), channel_id=1, source_target_pairs={{1,2},{2,1},{5,6},{6,5},{9,10},{10,9},{13,14},{14,13},{17,18},{18,... | collective-permute-start | bytes 3956744 | tf_op jit(solution)/shard_map/ppermute | solution.py:67
  77.8 44.1 %collective-permute-start.11 = (bf16[4,2,2,192,384]{4,3,2,1,0:T(8,128)(2,1)}, bf16[4,2,2,192,384]{4,3,2,1,0:T(8,128)(2,1)}, u32[]{:S(2)}, u32[]{:S(2)}) collective-permute-start(bf16[4,2,2,192,384]{4,3,2,1,0:T(8,128)(2,1)} %maximum_maximum_fusion.1), channel_id=1, source_target_pairs={{0,4},{4,0},{8,12},{12,8},{16,20},{20,16},{24,28},{28,24},{1,5},{5... | collective-permute-start | bytes 7077896 | tf_op jit(solution)/shard_map/ppermute | solution.py:64
  106.9 146.7 %collective-permute-start.29 = (bf16[1,2,368,896]{3,2,1,0:T(8,128)(2,1)}, bf16[1,2,368,896]{3,2,1,0:T(8,128)(2,1)}, u32[]{:S(2)}, u32[]{:S(2)}) collective-permute-start(bf16[1,2,368,896]{3,2,1,0:T(8,128)(2,1)} %pad_maximum_fusion.13), channel_id=1, source_target_pairs={{0,16},{4,20},{8,24},{12,28},{16,0},{20,4},{24,8},{28,12},{1,17},{... | collective-permute-start | bytes 3956744 | tf_op jit(solution)/shard_map/ppermute | solution.py:64
  116.0 152.1 %collective-permute-start.33 = (bf16[1,2,368,896]{3,2,1,0:T(8,128)(2,1)}, bf16[1,2,368,896]{3,2,1,0:T(8,128)(2,1)}, u32[]{:S(2)}, u32[]{:S(2)}) collective-permute-start(bf16[1,2,368,896]{3,2,1,0:T(8,128)(2,1)} %pad_maximum_fusion.14), channel_id=1, source_target_pairs={{0,8},{4,12},{8,0},{12,4},{16,24},{20,28},{24,16},{28,20},{1,9},{5... | collective-permute-start | bytes 3956744 | tf_op jit(solution)/shard_map/ppermute | solution.py:64
  121.9 43.1 %collective-permute-start.21 = (bf16[2,2,184,896]{3,2,1,0:T(8,128)(2,1)}, bf16[2,2,184,896]{3,2,1,0:T(8,128)(2,1)}, u32[]{:S(2)}, u32[]{:S(2)}) collective-permute-start(bf16[2,2,184,896]{3,2,1,0:T(8,128)(2,1)} %get-tuple-element.82), channel_id=1, source_target_pairs={{0,4},{4,0},{8,12},{12,8},{16,20},{20,16},{24,28},{28,24},{1,5},{5... | collective-permute-start | bytes 3956744 | tf_op jit(solution)/shard_map/ppermute | solution.py:64
  143.8 34.2 %collective-permute-start.13 = (bf16[512,768]{1,0:T(8,128)(2,1)S(1)}, bf16[512,768]{1,0:T(8,128)(2,1)}, u32[]{:S(2)}, u32[]{:S(2)}) collective-permute-start(bf16[512,768]{1,0:T(8,128)(2,1)S(1)} %copy.291.kv_ref), channel_id=1, source_target_pairs={{0,1},{1,2},{2,3},{4,5},{5,6},{6,7},{8,9},{9,10},{10,11},{12,13},{... | collective-permute-start | bytes 2359304 | tf_op jit(solution)/shard_map/ppermute | solution.py:67
  165.0 28.2 %collective-permute-start.15 = (bf16[288,768]{1,0:T(8,128)(2,1)S(1)}, bf16[288,768]{1,0:T(8,128)(2,1)S(1)}, u32[]{:S(2)}, u32[]{:S(2)}) collective-permute-start(bf16[288,768]{1,0:T(8,128)(2,1)S(1)} %copy.292), channel_id=1, source_target_pairs={{2,0},{3,1},{6,4},{7,5},{10,8},{11,9},{14,12},{15,13},{18,16},{19,... | collective-permute-start | bytes 1327112 | tf_op jit(solution)/shard_map/ppermute | solution.py:67
  178.0 65.1 %collective-permute-start.36 = (bf16[288,384]{1,0:T(8,128)(2,1)}, bf16[288,384]{1,0:T(8,128)(2,1)}, u32[]{:S(2)}, u32[]{:S(2)}) collective-permute-start(bf16[288,384]{1,0:T(8,128)(2,1)} %copy.294), channel_id=1, source_target_pairs={{0,2},{1,3},{4,6},{5,7},{8,10},{9,11},{12,14},{13,15},{16,18},{17,... | collective-permute-start | bytes 663560 | tf_op jit(solution)/shard_map/ppermute | solution.py:67
  184.1 38.1 %collective-permute-start.30 = (bf16[2,368,896]{2,1,0:T(8,128)(2,1)}, bf16[2,368,896]{2,1,0:T(8,128)(2,1)}, u32[]{:S(2)}, u32[]{:S(2)}) collective-permute-start(bf16[2,368,896]{2,1,0:T(8,128)(2,1)} %bitcast.70), channel_id=1, source_target_pairs={{0,16},{4,20},{8,24},{12,28},{16,0},{20,4},{24,8},{28,12},{1,17},{... | collective-permute-start | bytes 3956744 | tf_op jit(solution)/shard_map/ppermute | solution.py:64
  193.2 45.6 %collective-permute-start.22 = (bf16[2,368,896]{2,1,0:T(8,128)(2,1)}, bf16[2,368,896]{2,1,0:T(8,128)(2,1)}, u32[]{:S(2)}, u32[]{:S(2)}) collective-permute-start(bf16[2,368,896]{2,1,0:T(8,128)(2,1)} %bitcast.43), channel_id=1, source_target_pairs={{0,8},{4,12},{8,0},{12,4},{16,24},{20,28},{24,16},{28,20},{1,9},{5... | collective-permute-start | bytes 3956744 | tf_op jit(solution)/shard_map/ppermute | solution.py:64
  227.6 65.9 %collective-permute-start.31 = (bf16[2,2,368,896]{3,2,0,1:T(8,128)(2,1)}, bf16[2,2,368,896]{3,2,0,1:T(8,128)(2,1)}, u32[]{:S(2)}, u32[]{:S(2)}) collective-permute-start(bf16[2,2,368,896]{3,2,0,1:T(8,128)(2,1)} %pad_maximum_fusion.9), channel_id=1, source_target_pairs={{0,8},{4,12},{8,0},{12,4},{16,24},{20,28},{24,16},{28,20},{1,9},{5... | collective-permute-start | bytes 7913480 | tf_op jit(solution)/shard_map/ppermute | solution.py:64
  238.8 38.6 %collective-permute-start.16 = (bf16[512,1472]{0,1:T(8,128)(2,1)}, bf16[512,1472]{0,1:T(8,128)(2,1)}, u32[]{:S(2)}, u32[]{:S(2)}) collective-permute-start(bf16[512,1472]{0,1:T(8,128)(2,1)} %multiply_convert_fusion), channel_id=1, source_target_pairs={{0,4},{4,0},{8,12},{12,8},{16,20},{20,16},{24,28},{28,24},{1,5},{5... | collective-permute-start | bytes 4521992 | tf_op jit(solution)/shard_map/ppermute | solution.py:64
  243.1 59.9 %collective-permute-start.23 = (bf16[2,2,368,896]{3,2,0,1:T(8,128)(2,1)}, bf16[2,2,368,896]{3,2,0,1:T(8,128)(2,1)}, u32[]{:S(2)}, u32[]{:S(2)}) collective-permute-start(bf16[2,2,368,896]{3,2,0,1:T(8,128)(2,1)} %pad_maximum_fusion.7), channel_id=1, source_target_pairs={{0,16},{4,20},{8,24},{12,28},{16,0},{20,4},{24,8},{28,12},{1,17},{... | collective-permute-start | bytes 7913480 | tf_op jit(solution)/shard_map/ppermute | solution.py:64
  268.1 143.5 %collective-permute-start.38 = (bf16[512,384]{1,0:T(8,128)(2,1)S(1)}, bf16[512,384]{1,0:T(8,128)(2,1)}, u32[]{:S(2)}, u32[]{:S(2)}) collective-permute-start(bf16[512,384]{1,0:T(8,128)(2,1)S(1)} %copy-done.51), channel_id=1, source_target_pairs={{1,0},{2,1},{3,2},{5,4},{6,5},{7,6},{9,8},{10,9},{11,10},{13,12},{... | collective-permute-start | bytes 1179656 | tf_op jit(solution)/shard_map/ppermute | solution.py:67
  275.3 138.3 %collective-permute-start.39 = (bf16[288,384]{1,0:T(8,128)(2,1)}, bf16[288,384]{1,0:T(8,128)(2,1)}, u32[]{:S(2)}, u32[]{:S(2)}) collective-permute-start(bf16[288,384]{1,0:T(8,128)(2,1)} %copy.295), channel_id=1, source_target_pairs={{2,0},{3,1},{6,4},{7,5},{10,8},{11,9},{14,12},{15,13},{18,16},{19,... | collective-permute-start | bytes 663560 | tf_op jit(solution)/shard_map/ppermute | solution.py:67
  458.7 61.9 %collective-permute-start.41 = (bf16[512,384]{1,0:T(8,128)(2,1)}, bf16[512,384]{1,0:T(8,128)(2,1)}, u32[]{:S(2)}, u32[]{:S(2)}) collective-permute-start(bf16[512,384]{1,0:T(8,128)(2,1)} %copy.257.do_ref), channel_id=1, source_target_pairs={{0,1},{1,2},{2,3},{4,5},{5,6},{6,7},{8,9},{9,10},{10,11},{12,13},{... | collective-permute-start | bytes 1179656 | tf_op jit(solution)/shard_map/ppermute | solution.py:67
  476.2 36.8 %collective-permute-start.45 = (f32[512,16]{1,0:T(8,128)}, f32[512,16]{1,0:T(8,128)}, u32[]{:S(2)}, u32[]{:S(2)}) collective-permute-start(f32[512,16]{1,0:T(8,128)} %slice.346), channel_id=1, source_target_pairs={{0,1},{1,2},{2,3},{4,5},{5,6},{6,7},{8,9},{9,10},{10,11},{12,13},{... | collective-permute-start | bytes 98312 | tf_op jit(solution)/shard_map/ppermute | solution.py:67
  483.2 35.4 %collective-permute-start.40 = (bf16[288,384]{1,0:T(8,128)(2,1)}, bf16[288,384]{1,0:T(8,128)(2,1)S(1)}, u32[]{:S(2)}, u32[]{:S(2)}) collective-permute-start(bf16[288,384]{1,0:T(8,128)(2,1)} %copy.286), channel_id=1, source_target_pairs={{0,2},{1,3},{4,6},{5,7},{8,10},{9,11},{12,14},{13,15},{16,18},{17,... | collective-permute-start | bytes 663560 | tf_op jit(solution)/shard_map/ppermute | solution.py:67
  513.1 86.6 %collective-permute-start.55 = (bf16[3,2,368,896]{3,2,1,0:T(8,128)(2,1)}, bf16[3,2,368,896]{3,2,1,0:T(8,128)(2,1)}, u32[]{:S(2)}, u32[]{:S(2)}) collective-permute-start(bf16[3,2,368,896]{3,2,1,0:T(8,128)(2,1)} %dynamic-slice_bitcast_fusion.1), channel_id=1, source_target_pairs={{0,16},{4,20},{8,24},{12,28},{16,0},{20,4},{24,8},{28,12},{1,17},{... | collective-permute-start | bytes 11870216 | tf_op jit(solution)/shard_map/ppermute | solution.py:64
  514.2 93.2 %collective-permute-start.60 = (bf16[3,2,368,896]{3,2,1,0:T(8,128)(2,1)}, bf16[3,2,368,896]{3,2,1,0:T(8,128)(2,1)}, u32[]{:S(2)}, u32[]{:S(2)}) collective-permute-start(bf16[3,2,368,896]{3,2,1,0:T(8,128)(2,1)} %dynamic-slice_bitcast_fusion), channel_id=1, source_target_pairs={{0,8},{4,12},{8,0},{12,4},{16,24},{20,28},{24,16},{28,20},{1,9},{5... | collective-permute-start | bytes 11870216 | tf_op jit(solution)/shard_map/ppermute | solution.py:64
  583.1 31.1 %collective-permute-start.48 = (bf16[4,2,2,192,384]{4,3,2,1,0:T(8,128)(2,1)}, bf16[4,2,2,192,384]{4,3,2,1,0:T(8,128)(2,1)}, u32[]{:S(2)}, u32[]{:S(2)}) collective-permute-start(bf16[4,2,2,192,384]{4,3,2,1,0:T(8,128)(2,1)} %dynamic-slice_bitcast_fusion.2), channel_id=1, source_target_pairs={{0,4},{4,0},{8,12},{12,8},{16,20},{20,16},{24,28},{28,24},{1,5},{5... | collective-permute-start | bytes 7077896 | tf_op jit(solution)/shard_map/ppermute | solution.py:64
  607.4 67.2 %collective-permute-start.56 = (bf16[3,368,896]{2,1,0:T(8,128)(2,1)}, bf16[3,368,896]{2,1,0:T(8,128)(2,1)}, u32[]{:S(2)}, u32[]{:S(2)}) collective-permute-start(bf16[3,368,896]{2,1,0:T(8,128)(2,1)} %dynamic-slice_bitcast_fusion.4), channel_id=1, source_target_pairs={{0,8},{4,12},{8,0},{12,4},{16,24},{20,28},{24,16},{28,20},{1,9},{5... | collective-permute-start | bytes 5935112 | tf_op jit(solution)/shard_map/ppermute | solution.py:64
  613.9 63.1 %collective-permute-start.61 = (bf16[3,368,896]{2,1,0:T(8,128)(2,1)}, bf16[3,368,896]{2,1,0:T(8,128)(2,1)}, u32[]{:S(2)}, u32[]{:S(2)}) collective-permute-start(bf16[3,368,896]{2,1,0:T(8,128)(2,1)} %dynamic-slice_bitcast_fusion.3), channel_id=1, source_target_pairs={{0,16},{4,20},{8,24},{12,28},{16,0},{20,4},{24,8},{28,12},{1,17},{... | collective-permute-start | bytes 5935112 | tf_op jit(solution)/shard_map/ppermute | solution.py:64
  617.9 51.8 %collective-permute-start.49 = (bf16[2,2,192,384]{3,2,1,0:T(8,128)(2,1)}, bf16[2,2,192,384]{3,2,1,0:T(8,128)(2,1)}, u32[]{:S(2)}, u32[]{:S(2)}) collective-permute-start(bf16[2,2,192,384]{3,2,1,0:T(8,128)(2,1)} %dynamic-slice_bitcast_fusion.8), channel_id=1, source_target_pairs={{0,16},{4,20},{8,24},{12,28},{16,0},{20,4},{24,8},{28,12},{1,17},{... | collective-permute-start | bytes 1769480 | tf_op jit(solution)/shard_map/ppermute | solution.py:64
  620.4 52.1 %collective-permute-start.51 = (bf16[2,2,192,384]{3,2,1,0:T(8,128)(2,1)}, bf16[2,2,192,384]{3,2,1,0:T(8,128)(2,1)}, u32[]{:S(2)}, u32[]{:S(2)}) collective-permute-start(bf16[2,2,192,384]{3,2,1,0:T(8,128)(2,1)} %dynamic-slice_bitcast_fusion.7), channel_id=1, source_target_pairs={{0,8},{4,12},{8,0},{12,4},{16,24},{20,28},{24,16},{28,20},{1,9},{5... | collective-permute-start | bytes 1769480 | tf_op jit(solution)/shard_map/ppermute | solution.py:64
  682.7 102.0 %collective-permute-start.58 = (bf16[3,184,896]{2,1,0:T(8,128)(2,1)}, bf16[3,184,896]{2,1,0:T(8,128)(2,1)}, u32[]{:S(2)}, u32[]{:S(2)}) collective-permute-start(bf16[3,184,896]{2,1,0:T(8,128)(2,1)} %fusion.44), channel_id=1, source_target_pairs={{0,2},{2,0},{1,3},{3,1},{4,6},{6,4},{5,7},{7,5},{8,10},{10,8},{9,1... | collective-permute-start | bytes 2967560 | tf_op jit(solution)/shard_map/ppermute | solution.py:67
  688.2 103.4 %collective-permute-start.63 = (bf16[3,184,896]{2,1,0:T(8,128)(2,1)}, bf16[3,184,896]{2,1,0:T(8,128)(2,1)}, u32[]{:S(2)}, u32[]{:S(2)}) collective-permute-start(bf16[3,184,896]{2,1,0:T(8,128)(2,1)} %fusion.40), channel_id=1, source_target_pairs={{0,2},{2,0},{1,3},{3,1},{4,6},{6,4},{5,7},{7,5},{8,10},{10,8},{9,1... | collective-permute-start | bytes 2967560 | tf_op jit(solution)/shard_map/ppermute | solution.py:67
  689.0 93.3 %collective-permute-start.53 = (bf16[2,192,384]{2,1,0:T(8,128)(2,1)}, bf16[2,192,384]{2,1,0:T(8,128)(2,1)S(1)}, u32[]{:S(2)}, u32[]{:S(2)}) collective-permute-start(bf16[2,192,384]{2,1,0:T(8,128)(2,1)} %dynamic-slice_bitcast_fusion.9), channel_id=1, source_target_pairs={{0,2},{2,0},{1,3},{3,1},{4,6},{6,4},{5,7},{7,5},{8,10},{10,8},{9,1... | collective-permute-start | bytes 884744 | tf_op jit(solution)/shard_map/ppermute | solution.py:67
  (112 other events, 1683.1 us)

commit v2 on v1

v2 whole, which is shorter than its diff:
```python
import math
from functools import partial

import jax
import jax.numpy as jnp
import numpy as np
from jax import lax
from jax.experimental import pallas as pl
from jax.experimental.pallas import tpu as pltpu
from jax.sharding import PartitionSpec as P

HEADS = 6
BUCKETS = 32
MAX_DOC = 800
BLK = 256
SPAN = 1024
EPS = 1e-06
MASKED = -1e30
F32 = jnp.float32
BF16 = jnp.bfloat16
VMEM_CAP = 58 * 1024 * 1024
LANES = 128
GELU_K = math.sqrt(2.0 / math.pi)
GELU_A = 0.044715


def bucket_table():
    relative = np.arange(SPAN) - SPAN // 2
    distance = np.abs(relative)
    steps = np.array([12, 16, 23, 32, 46, 64, 91])
    levels = (distance[:, None] >= steps[None, :]).sum(axis=1)
    inside = np.where(distance < 8, distance, 8 + levels)
    return (inside + 16 * (relative > 0)).astype(np.int32)


class Moves:
    def __init__(self, n_dp, n_seq):
        self.n_dp, self.n_seq = n_dp, n_seq
        plane = n_dp // 2
        side = int(round(math.sqrt(plane)))
        self.size = {"a": plane // side, "b": side, "c": 2, "z": n_seq}
        dp = lax.axis_index("dp")
        self.last = {}
        self.index = {
            "a": dp // (2 * side),
            "b": (dp // 2) % side,
            "c": dp % 2,
            "z": lax.axis_index("seq"),
        }

    def rotate(self, x, axis):
        n = self.size[axis]
        if axis == "z":
            return lax.ppermute(x, "seq", [(i, (i + 1) % n) for i in range(n)])
        pairs = []
        side = self.size["b"]
        for i in range(self.n_dp):
            a, b, c = i // (2 * side), (i // 2) % side, i % 2
            if axis == "a":
                a = (a + 1) % n
            elif axis == "b":
                b = (b + 1) % n
            else:
                c = 1 - c
            pairs.append((i, (a * side + b) * 2 + c))
        return lax.ppermute(x, "dp", pairs)

    def zperm(self, x, pairs):
        return lax.ppermute(x, "seq", pairs)

    def same_core(self):
        return [list(range(c, self.n_dp, 2)) for c in range(2)]

    def ring(self, x, waits=()):
        parts = []
        for step in range(self.n_seq - 1):
            x = self.rotate(after(x, *waits[step]) if step < len(waits) else x, "z")
            parts.append(x)
        return parts

    def gather(self, x, axis, at=0):
        n, i = self.size[axis], self.index[axis]
        if n == 2:
            other = self.rotate(x, axis)
            return ordered(i == 0, x, other, at)
        parts = [x]
        for _ in range(n - 1):
            parts.append(self.rotate(parts[-1], axis))
        turned = jnp.stack(parts[::-1] + parts[::-1], 0)
        full = lax.dynamic_slice_in_dim(turned, n - 1 - i, n, 0)
        return jnp.moveaxis(full, 0, at)

    def scatter(self, x, axis, at=0, out=BF16):
        n, i = self.size[axis], self.index[axis]
        take = lambda k: lax.dynamic_index_in_dim(x, k, at, keepdims=False)
        if n == 2:
            other = self.rotate(take(1 - i), axis)
            return add(take(i), other, out)
        acc = take((i + n - 1) % n)
        for step in range(n - 1):
            got = self.rotate(acc, axis)
            last = step == n - 2
            acc = add(take((i + 2 * n - 2 - step) % n), got, out if last else BF16)
        return acc


def after(x, *others):
    others = [o for o in others if o is not None]
    return lax.optimization_barrier((x, *others))[0] if others else x


def add(x, y, out):
    return (x.astype(F32) + y.astype(F32)).astype(out)


def ordered(first, x, y, at):
    return jnp.stack([jnp.where(first, x, y), jnp.where(first, y, x)], at)


def z_gather(mv, w, waits=()):
    z, n = mv.index["z"], mv.n_seq
    blocks = [w] + mv.ring(w, waits)
    turned = jnp.stack(blocks[::-1] + blocks[::-1], 0)
    return lax.dynamic_slice_in_dim(turned, n - 1 - z, n, 0)


def small_plane(mv):
    return mv.size["a"] == 2 and mv.size["b"] == 2 and mv.n_seq == 4


def gather_core(mv, w, ready):
    k, rows, cols = w.shape
    c = mv.index["c"]
    full = lax.all_gather(w, "seq")
    zh = mv.n_seq // 2
    keep = lax.dynamic_slice_in_dim(full, c * zh, zh, 0)
    send = lax.dynamic_slice_in_dim(full, (1 - c) * zh, zh, 0)
    recv = mv.rotate(after(send, *ready), "c")
    block = ordered(c == 0, keep, recv, 2)
    return [block[j].reshape(k, 2 * rows, cols) for j in range(zh)]


GROUPS = ((0, 1), (2,))


def scatter_plane(mv, grad):
    quarter, k, rows, cols = grad.shape
    chips = mv.n_dp // 2
    x = grad
    if chips != quarter:
        x = jnp.moveaxis(grad, 1, 0).reshape(k, chips, quarter * rows // chips, cols)
        x = jnp.moveaxis(x, 0, 1)
    x = lax.psum_scatter(x, "dp", scatter_dimension=0, axis_index_groups=mv.same_core())
    x = x.reshape(k, 2, x.shape[1] // 2, cols)
    return x


def swap_cores(mv, x):
    c = mv.index["c"]
    take = lambda i: lax.dynamic_index_in_dim(x, i, 1, keepdims=False)
    return take(c), mv.rotate(take(1 - c), "c")


class ZSum:
    def __init__(self, mv, j, x):
        self.mv, self.j, self.x = mv, j, x

    def swap(self, wait):
        c = self.mv.index["c"]
        x = after(self.x, wait)
        take = lambda i: lax.dynamic_index_in_dim(x, i, 1, keepdims=False)
        mine, other = take(c), self.mv.rotate(take(1 - c), "c")
        here = (self.mv.index["z"] // 2) == c
        self.pair = mine, other
        self.near, self.far = jnp.where(here, mine, other), jnp.where(here, other, mine)
        return other

    def inwards(self, wait=None):
        got = self.mv.zperm(after(self.far, wait), [(0, 1), (3, 2)])
        self.far = add(self.far, got, BF16)
        return got

    def across(self, wait=None):
        got = self.mv.zperm(after(self.far, wait), [(1, 2), (2, 1)])
        self.near = add(self.near, got, BF16)
        return got

    def home(self, wait=None):
        j = self.j
        got = self.mv.zperm(after(self.near, wait), [(1 - j, j), (3 - j, 2 + j)])
        self.total = add(self.near, got, F32)
        return got


def z_totals(mv, sums):
    z, c = mv.index["z"], mv.index["c"]
    result = []
    for g in range(len(GROUPS)):
        units = [groups[g] for groups in sums]
        if mv.n_seq == 4:
            result.append(jnp.where(z % 2 == 0, units[0].total, units[1].total))
        else:
            full = jnp.stack([ordered(c == 0, *u.pair, 0) for u in units], 1)
            result.append(mv.scatter(full.reshape((mv.n_seq,) + units[0].pair[0].shape), "z", 0, F32))
    return result


def gather_small(mv, w):
    full = z_gather(mv, w)
    half = mv.n_seq // 2
    lo_one = mv.gather(full[:half], "b", 1)
    hi_one = mv.gather(full[half:], "a", 1)
    lo = mv.gather(lo_one, "a", 1)
    hi = mv.gather(hi_one, "b", 2)
    both = jnp.concatenate([lo, hi], 0)
    both = mv.gather(both, "c", 3)
    return both.reshape((mv.n_seq, mv.n_dp) + w.shape), (full, (lo_one, hi_one), (lo, hi))


def scatter_small(mv, g, between):
    na, nb = mv.size["a"], mv.size["b"]
    zs, _, rp, cols = g.shape
    x = g.reshape(zs, na, nb, 2, rp, cols)
    x = mv.scatter(x, "c", 3)
    half = zs // 2
    x = after(x, *between())
    lo = mv.scatter(mv.scatter(x[:half], "a", 1), "b", 1)
    hi = mv.scatter(mv.scatter(x[half:], "b", 2), "a", 1)
    x = jnp.concatenate([lo, hi], 0)
    return mv.scatter(x, "z", 0, F32), (lo, hi)


def reach_of(rows, n_seq):
    need, parts = MAX_DOC - 1, []
    while need > 0 and len(parts) + 1 < n_seq:
        parts.append(min(rows, -(-need // LANES) * LANES))
        need -= rows
    return parts


def halo(mv, x, waits=()):
    rows, n = x.shape[1], mv.n_seq
    left, right = [], []
    x_own = x
    for hop, cols in enumerate(reach_of(rows, n)):
        step = hop + 1
        if hop > 0:
            x = after(x, left[0], right[-1], *waits)
        left.insert(0, mv.zperm(x[:, rows - cols :], [(i, i + step) for i in range(n - step)]))
        right.append(mv.zperm(x[:, :cols], [(i + step, i) for i in range(n - step)]))
    return left + [x_own] + right


def dot(x, y, dims):
    return lax.dot_general(x, y, (dims, ((), ())), preferred_element_type=F32)


def nt(x, y):
    return dot(x, y, ((1,), (1,)))


def nn(x, y):
    return dot(x, y, ((1,), (0,)))


def tn(x, y):
    return dot(x, y, ((0,), (0,)))


def make_tiles(vec_ref, tiles):
    for h in range(HEADS):
        line = vec_ref[h : h + 1, :]
        wide = jnp.broadcast_to(line, (BLK, SPAN))
        rolled = pltpu.roll(wide, 0, 1, stride=1, stride_axis=0)
        tiles[h * 5] = jnp.broadcast_to(line[:, :1], (BLK, BLK))
        tiles[h * 5 + 4] = jnp.broadcast_to(line[:, SPAN - 1 :], (BLK, BLK))
        for d in (-1, 0, 1):
            at = SPAN // 2 + BLK * d
            tiles[h * 5 + 2 + d] = rolled[:, at : at + BLK]


def class_of(query_block, key_block):
    return jnp.clip(query_block - key_block, -2, 2) + 2


def lay_out(off, pieces, whole):
    middle = len(pieces) // 2
    at = off - sum(p.shape[1] for p in pieces[:middle])
    if at > 0:
        whole[:, :at] = jnp.zeros((whole.shape[0], at), whole.dtype)
    for p in pieces:
        whole[:, at : at + p.shape[1]] = p[...]
        at += p.shape[1]
    if at < whole.shape[1]:
        whole[:, at:] = jnp.zeros((whole.shape[0], whole.shape[1] - at), whole.dtype)


def block_at(k):
    return pl.ds(pl.multiple_of(k * BLK, BLK), BLK)


def forward_kernel(off, count, lohi, vec, q_ref, segq, segk, *rest):
    pieces = rest[:count]
    out, exact, lse, split, tiles, kv = rest[count:]
    i = pl.program_id(0)

    @pl.when(i == 0)
    def _():
        make_tiles(vec, tiles)
        lay_out(off, pieces, kv)

    own = off // BLK + i
    inner = HEADS * 64
    low, high = lohi[i, 0], lohi[i, 1]
    seg_row = segq[0]
    split[...] = jnp.zeros_like(split)
    lse[...] = jnp.zeros_like(lse)
    for pair in range(HEADS // 2):
        heads = (2 * pair, 2 * pair + 1)
        qs = [q_ref[h * 64 : h * 64 + 64, :] for h in heads]

        def body(kb, state):
            cols = block_at(kb)
            same = segk[cols, :] == seg_row
            kind = class_of(own, kb)
            new = []
            for e, h in enumerate(heads):
                peak, total, acc = state[e]
                s = tn(kv[h * 64 : h * 64 + 64, cols], qs[e]) + tiles[h * 5 + kind]
                s = jnp.where(same, s, MASKED)
                top = jnp.maximum(peak, jnp.max(s, axis=0, keepdims=True))
                fade = jnp.exp(peak - top)
                p = jnp.exp(s - top)
                total = total * fade + jnp.sum(p, axis=0, keepdims=True)
                acc = acc * fade + nn(kv[inner + h * 64 : inner + h * 64 + 64, cols], p.astype(BF16))
                new.append((top, total, acc))
            return tuple(new)

        start = (
            jnp.full((1, BLK), MASKED, F32),
            jnp.zeros((1, BLK), F32),
            jnp.zeros((64, BLK), F32),
        )
        state = lax.fori_loop(low, high, body, (start, start))
        for e, h in enumerate(heads):
            peak, total, acc = state[e]
            done = acc / total
            out[h * 64 : h * 64 + 64, :] = done.astype(BF16)
            exact[h * 64 : h * 64 + 64, :] = done
            log = peak + jnp.log(total)
            lse[h : h + 1, :] = log
            for part in range(3):
                piece = log.astype(BF16)
                split[part * 8 + h : part * 8 + h + 1, :] = piece
                log = log - piece.astype(F32)


def query_kernel(off, count, lohi, vec, q_ref, do_ref, lse, delta, segq, segk, *rest):
    pieces = rest[:count]
    dq, near, far, tiles, sums, kv = rest[count:]
    i = pl.program_id(0)

    @pl.when(i == 0)
    def _():
        make_tiles(vec, tiles)
        lay_out(off, pieces, kv)
        sums[...] = jnp.zeros_like(sums)

    own = off // BLK + i
    inner = HEADS * 64
    low, high = lohi[i, 0], lohi[i, 1]
    seg_row = segq[0]
    for pair in range(HEADS // 2):
        heads = (2 * pair, 2 * pair + 1)
        qs = [q_ref[h * 64 : h * 64 + 64, :] for h in heads]
        dos = [do_ref[h * 64 : h * 64 + 64, :] for h in heads]

        def body(kb, state):
            cols = block_at(kb)
            same = segk[cols, :] == seg_row
            kind = class_of(own, kb)
            new = []
            for e, h in enumerate(heads):
                keys = kv[h * 64 : h * 64 + 64, cols]
                s = tn(keys, qs[e]) + tiles[h * 5 + kind]
                s = jnp.where(same, s, MASKED)
                p = jnp.exp(s - lse[h : h + 1, :])
                dp = tn(kv[inner + h * 64 : inner + h * 64 + 64, cols], dos[e])
                ds = p * (dp - delta[h : h + 1, :])
                at = h * 5 + kind
                sums[at] = sums[at] + ds
                new.append(state[e] + nn(keys, ds.astype(BF16)))
            return tuple(new)

        start = jnp.zeros((64, BLK), F32)
        state = lax.fori_loop(low, high, body, (start, start))
        for e, h in enumerate(heads):
            dq[h * 64 : h * 64 + 64, :] = state[e].astype(BF16)

    @pl.when(i == pl.num_programs(0) - 1)
    def _():
        for h in range(HEADS):
            zero = jnp.zeros((BLK, BLK), F32)
            x = jnp.concatenate([sums[h * 5 + 1], sums[h * 5 + 2], sums[h * 5 + 3], zero], axis=1)
            n = BLK // 2
            while n >= 8:
                x = x[:n] + pltpu.roll(x[n:], SPAN - n, 1)
                n //= 2
            row = lax.broadcasted_iota(jnp.int32, x.shape, 0)
            for n in (4, 2, 1):
                x = jnp.where((row & n) != 0, pltpu.roll(x, SPAN - n, 1), x)
            near[h] = x
            far[h, 0] = jnp.sum(sums[h * 5].reshape(BLK // 8, 8, BLK), axis=0)
            far[h, 1] = jnp.sum(sums[h * 5 + 4].reshape(BLK // 8, 8, BLK), axis=0)


def key_kernel(off, count, lohi, vec, k_ref, v_ref, segq, segk, *rest):
    queries, answers = rest[:count], rest[count : 2 * count]
    dk, dv, tiles, qs, dos = rest[2 * count :]
    i = pl.program_id(0)

    @pl.when(i == 0)
    def _():
        make_tiles(vec, tiles)
        lay_out(off, queries, qs)
        lay_out(off, answers, dos)

    own = off // BLK + i
    inner = HEADS * 64
    low, high = lohi[i, 0], lohi[i, 1]
    seg_col = segk[...]
    for pair in range(HEADS // 2):
        heads = (2 * pair, 2 * pair + 1)
        ks = [k_ref[h * 64 : h * 64 + 64, :] for h in heads]
        vs = [v_ref[h * 64 : h * 64 + 64, :] for h in heads]

        def body(qb, state):
            cols = block_at(qb)
            same = seg_col == segq[qb]
            kind = class_of(qb, own)
            logs = qs[inner : inner + 8, cols].astype(F32)
            logs = logs + qs[inner + 8 : inner + 16, cols].astype(F32)
            logs = logs + qs[inner + 16 : inner + 24, cols].astype(F32)
            deltas = dos[inner : inner + 8, cols].astype(F32)
            deltas = deltas + dos[inner + 8 : inner + 16, cols].astype(F32)
            new = []
            for e, h in enumerate(heads):
                q, do = qs[h * 64 : h * 64 + 64, cols], dos[h * 64 : h * 64 + 64, cols]
                s = tn(ks[e], q) + tiles[h * 5 + kind]
                s = jnp.where(same, s, MASKED)
                p = jnp.exp(s - logs[h : h + 1, :])
                ds = p * (tn(vs[e], do) - deltas[h : h + 1, :])
                to_k, to_v = state[e]
                new.append((to_k + nt(q, ds.astype(BF16)), to_v + nt(do, p.astype(BF16))))
            return tuple(new)

        start = jnp.zeros((64, BLK), F32)
        state = lax.fori_loop(low, high, body, ((start, start), (start, start)))
        for e, h in enumerate(heads):
            dk[h * 64 : h * 64 + 64, :] = state[e][0].astype(BF16)
            dv[h * 64 : h * 64 + 64, :] = state[e][1].astype(BF16)


def whole_block(shape):
    return pl.BlockSpec(shape, lambda i: (0,) * len(shape))


def col_block(rows):
    return pl.BlockSpec((rows, BLK), lambda i: (0, i))


SMEM_SPEC = pl.BlockSpec(memory_space=pltpu.SMEM)
COL_SEGS = pl.BlockSpec((BLK, 1), lambda i: (i, 0))
ROW_SEGS = pl.BlockSpec((1, 1, BLK), lambda i: (i, 0, 0))
TILES = pltpu.VMEM((HEADS * 5, BLK, BLK), F32)
LIGHT = pl.CostEstimate(flops=10**9, bytes_accessed=8 * 2**20, transcendentals=0)


def params():
    return pltpu.CompilerParams(
        dimension_semantics=("arbitrary",), vmem_limit_bytes=VMEM_CAP
    )


def attend(off, span, lohi, vec, q, seg_row, seg_col, kv):
    inner, rows = q.shape
    return pl.pallas_call(
        partial(forward_kernel, off, len(kv)),
        grid=(rows // BLK,),
        in_specs=[SMEM_SPEC, whole_block(vec.shape), col_block(inner), ROW_SEGS, whole_block(seg_col.shape)]
        + [whole_block(p.shape) for p in kv],
        out_specs=[col_block(inner), col_block(inner), col_block(8), col_block(32)],
        out_shape=[
            jax.ShapeDtypeStruct((inner, rows), BF16),
            jax.ShapeDtypeStruct((inner, rows), F32),
            jax.ShapeDtypeStruct((8, rows), F32),
            jax.ShapeDtypeStruct((32, rows), BF16),
        ],
        scratch_shapes=[TILES, pltpu.VMEM((2 * inner, span), BF16)],
        cost_estimate=LIGHT,
        name="attend",
        compiler_params=params(),
    )(lohi, vec, q, seg_row, seg_col, *kv)


def attend_queries(off, span, lohi, vec, q, do, lse, delta, seg_row, seg_col, kv):
    inner, rows = q.shape
    return pl.pallas_call(
        partial(query_kernel, off, len(kv)),
        grid=(rows // BLK,),
        in_specs=[
            SMEM_SPEC,
            whole_block(vec.shape),
            col_block(inner),
            col_block(inner),
            col_block(8),
            col_block(8),
            ROW_SEGS,
            whole_block(seg_col.shape),
        ]
        + [whole_block(p.shape) for p in kv],
        out_specs=[
            col_block(inner),
            whole_block((HEADS, 8, SPAN)),
            whole_block((HEADS, 2, 8, BLK)),
        ],
        out_shape=[
            jax.ShapeDtypeStruct((inner, rows), BF16),
            jax.ShapeDtypeStruct((HEADS, 8, SPAN), F32),
            jax.ShapeDtypeStruct((HEADS, 2, 8, BLK), F32),
        ],
        scratch_shapes=[TILES, TILES, pltpu.VMEM((2 * inner, span), BF16)],
        cost_estimate=LIGHT,
        name="attend_queries",
        compiler_params=params(),
    )(lohi, vec, q, do, lse, delta, seg_row, seg_col, *kv)


def attend_keys(off, span, lohi, vec, k, v, seg_row, seg_col, queries, answers):
    inner, rows = k.shape
    both = list(queries) + list(answers)
    return pl.pallas_call(
        partial(key_kernel, off, len(queries)),
        grid=(rows // BLK,),
        in_specs=[
            SMEM_SPEC,
            whole_block(vec.shape),
            col_block(inner),
            col_block(inner),
            whole_block(seg_row.shape),
            COL_SEGS,
        ]
        + [whole_block(p.shape) for p in both],
        out_specs=[col_block(inner), col_block(inner)],
        out_shape=[jax.ShapeDtypeStruct((inner, rows), BF16)] * 2,
        scratch_shapes=[
            TILES,
            pltpu.VMEM((queries[0].shape[0], span), BF16),
            pltpu.VMEM((answers[0].shape[0], span), BF16),
        ],
        cost_estimate=LIGHT,
        name="attend_keys",
        compiler_params=params(),
    )(lohi, vec, k, v, seg_row, seg_col, *both)


def ffn_kernel(nm, half, count, order, na, nb, ca, cb, nat, nbt, cat, cbt, *rest):
    pieces = rest[:count]
    out_a, out_b, gn_a, gn_b, *grads = rest[count : count + 4 + len(GROUPS)]
    weights, x, ct, hid, ggr, gur, sem = rest[count + 4 + len(GROUPS) :]
    i = pl.program_id(0)

    @pl.when(i == 0)
    def _():
        copies = []
        for piece in pieces:
            rows = piece.shape[2]
            for n in range(piece.shape[0]):
                k = len(copies) // 3
                at = pl.multiple_of(order[k], 16)
                for m in range(3):
                    copies.append(
                        pltpu.make_async_copy(
                            piece.at[n, m], weights.at[m, pl.ds(at, rows), :], sem.at[k, m]
                        )
                    )
        for copy in copies:
            copy.start()
        for copy in copies:
            copy.wait()

    @pl.when(i < half)
    def _():
        x[...] = na[...].T
        ct[...] = ca[...].T

    @pl.when((i >= half) & (i < nm))
    def _():
        x[...] = nb[...].T
        ct[...] = cb[...].T

    @pl.when(i < nm)
    def _():
        rows = pl.ds(pl.multiple_of(i * BLK, BLK), BLK)
        g = nn(x[...], weights[0])
        u = nn(x[...], weights[1])
        gh = nn(ct[...], weights[2])
        square = g * g
        t = jnp.tanh(GELU_K * g * (1.0 + GELU_A * square))
        part = 0.5 * (1.0 + t)
        gelu = g * part
        slope = part + 0.5 * g * (1.0 - t * t) * (GELU_K * (1.0 + 3.0 * GELU_A * square))
        h = (gelu * u).astype(BF16)
        gg = (gh * u * slope).astype(BF16)
        gu = (gh * gelu).astype(BF16)
        hid[rows, :] = h
        ggr[rows, :] = gg
        gur[rows, :] = gu
        out = nt(weights[2], h).astype(BF16)
        gn = (nt(weights[0], gg) + nt(weights[1], gu)).astype(BF16)

        @pl.when(i < half)
        def _():
            out_a[...] = out
            gn_a[...] = gn

        @pl.when(i >= half)
        def _():
            out_b[...] = out
            gn_b[...] = gn

    @pl.when(i >= nm)
    def _():
        t = hid.shape[0] // 2

        def product(first, second, right):
            return (nn(first[...], right[:t, :]) + nn(second[...], right[t:, :])).astype(BF16)

        lefts = ((nat, nbt, ggr), (nat, nbt, gur), (cat, cbt, hid))
        for g, members in enumerate(GROUPS):
            for n, m in enumerate(members):
                grads[g][0, n] = product(*lefts[m])


def ffn(n_own, n_other, c_own, c_other, pieces, starts):
    depth, t = n_own.shape
    cols = pieces[0].shape[3]
    half = t // BLK
    nm = 2 * half
    tile = depth // 4
    scalars = jnp.stack([jnp.asarray(v, jnp.int32) for v in starts])
    own = pl.BlockSpec((depth, BLK), lambda i, o: (0, jnp.minimum(i, half - 1)))
    other = pl.BlockSpec((depth, BLK), lambda i, o: (0, jnp.clip(i - half, 0, half - 1)))
    later = pl.BlockSpec((tile, t), lambda i, o: (jnp.maximum(i - nm, 0), 0))
    place = pl.BlockSpec(memory_space=pl.ANY)
    grads = [
        pl.BlockSpec((1, len(m), tile, cols), lambda i, o: (jnp.maximum(i - nm, 0), 0, 0, 0)) for m in GROUPS
    ]
    return pl.pallas_call(
        partial(ffn_kernel, nm, half, len(pieces)),
        grid_spec=pltpu.PrefetchScalarGridSpec(
            num_scalar_prefetch=1,
            grid=(nm + 4,),
            in_specs=[own, other, own, other, later, later, later, later] + [place] * len(pieces),
            out_specs=[own, other, own, other] + grads,
            scratch_shapes=[
                pltpu.VMEM((3, depth, cols), BF16),
                pltpu.VMEM((BLK, depth), BF16),
                pltpu.VMEM((BLK, depth), BF16),
                pltpu.VMEM((2 * t, cols), BF16),
                pltpu.VMEM((2 * t, cols), BF16),
                pltpu.VMEM((2 * t, cols), BF16),
                pltpu.SemaphoreType.DMA((len(starts), 3)),
            ],
        ),
        out_shape=[jax.ShapeDtypeStruct((depth, t), BF16)] * 4
        + [jax.ShapeDtypeStruct((4, len(m), tile, cols), BF16) for m in GROUPS],
        cost_estimate=LIGHT,
        name="ffn",
        compiler_params=params(),
    )(scalars, n_own, n_other, c_own, c_other, n_own, n_other, c_own, c_other, *pieces)


def rms_scale(x):
    return lax.rsqrt(jnp.mean(x * x, axis=0, keepdims=True) + EPS)


def norm_back(grad, x, scale, gain):
    gain_grad = jnp.sum(grad * (x * scale), axis=1)
    weighted = grad * gain
    dots = jnp.mean(weighted * x, axis=0, keepdims=True)
    return scale * weighted - x * (scale * scale * scale * dots), gain_grad


def on_device(
    n_dp,
    n_seq,
    inputs,
    segments,
    cotangent,
    w_query,
    w_key,
    w_value,
    w_out,
    w_gate,
    w_up,
    w_down,
    gain_attn,
    gain_ffn,
    rel_table,
):
    mv = Moves(n_dp, n_seq)
    seqs, rows, depth = inputs.shape
    source = inputs.reshape(seqs * rows, depth).T.astype(F32)
    tangent = cotangent.reshape(seqs * rows, depth).T
    rw, sc = w_query.shape
    inner = sc * n_seq
    wide = 4 * sc
    seg_rows = -(-rows // wide)
    rp = -(-(rw + 2 + seg_rows) // 16) * 16

    body = jnp.concatenate([w_query, w_key, w_value, w_out.T], axis=1)
    table_row = rel_table.reshape(-1)
    pad_to = lambda v: jnp.pad(v, (0, -v.shape[0] % wide)).reshape(-1, wide)
    packed = jnp.concatenate(
        [
            body,
            pad_to(jnp.concatenate([gain_attn, gain_ffn])),
            pad_to(table_row),
            pad_to(segments.reshape(rows).astype(BF16)),
            jnp.zeros((rp - rw - 2 - seg_rows, wide), BF16),
        ],
        axis=0,
    )
    att, stages = gather_small(mv, packed)
    full = att[:, :, :rw, :].reshape(n_seq, depth, wide)
    gain_one = att[0, :, rw, :rw].reshape(depth, 1).astype(F32)
    gain_two = att[0, :, rw, rw : 2 * rw].reshape(depth, 1).astype(F32)
    table = att[0, :, rw + 1, : table_row.shape[0]].reshape(BUCKETS, HEADS)
    here = lax.dynamic_index_in_dim(att, lax.axis_index("dp"), 1, keepdims=False)
    seg_seq = here[:, rw + 2 : rw + 2 + seg_rows, :].reshape(n_seq, -1)[:, :rows].astype(jnp.int32)

    scale_one = rms_scale(source)
    normed = ((source * scale_one) * gain_one).astype(BF16)
    qkv = jnp.einsum("zdc,dt->zct", full[:, :, : 3 * sc], normed, preferred_element_type=F32)
    qkv = jnp.transpose(qkv.astype(BF16).reshape(n_seq, 3, sc, rows), (1, 0, 2, 3))
    q = qkv[0].reshape(inner, rows)
    k = qkv[1].reshape(inner, rows)
    v = qkv[2].reshape(inner, rows)

    zh = n_seq // 2
    small = small_plane(mv)
    tangent_other = mv.rotate(tangent, "c")
    cores = gather_core(mv, jnp.stack([w_gate, w_up, w_down.T]), (q, tangent_other))
    kv_halo = halo(mv, after(jnp.concatenate([k, v], 0), cores[0]))
    pieces, starts = [], []
    for j in range(zh):
        full_block = lax.all_gather(cores[j], "dp", axis_index_groups=mv.same_core())
        if small:
            pieces.append([full_block])
            starts.append([jnp.int32(2 * rw * k) for k in range(4)])
        else:
            pieces.append([jnp.moveaxis(full_block, 0, 1).reshape(1, 3, depth, -1)])
            starts.append([jnp.int32(0)])

    off = -(-MAX_DOC // BLK) * BLK
    span = 2 * off + rows
    blocks = span // BLK
    seg_own = segments.reshape(rows)
    line = jnp.pad(seg_seq.reshape(-1), (off, off), constant_values=-1)
    seg_all = lax.dynamic_slice_in_dim(line, mv.index["z"] * rows, span, 0)
    seg_row = seg_all.reshape(blocks, 1, BLK)
    seg_col = seg_all.reshape(span, 1)
    own_row = seg_own.reshape(rows // BLK, 1, BLK)
    own_col = seg_own.reshape(rows, 1)
    spots = jnp.arange(span, dtype=jnp.int32)
    firsts = seg_own[::BLK]
    lasts = seg_own[BLK - 1 :: BLK]
    low = jnp.min(jnp.where(seg_all[None] == firsts[:, None], spots[None], 1 << 20), axis=1) // BLK
    high = jnp.max(jnp.where(seg_all[None] == lasts[:, None], spots[None], -1), axis=1) // BLK + 1
    lohi = jnp.stack([low, high], 1).astype(jnp.int32)

    buckets = bucket_table()
    buckets = np.concatenate([buckets[-1:], buckets[:0:-1]])
    chosen = jnp.asarray((buckets[:, None] == np.arange(BUCKETS)[None, :]), BF16)
    vec = dot(table, chosen, ((0,), (1,)))

    attended, exact, lse, lse_parts = attend(
        off, span, lohi, vec, q, own_row, seg_col, kv_halo
    )
    q_halo = halo(mv, jnp.concatenate([q, lse_parts], 0))

    mixed = source + jnp.einsum(
        "zdc,zct->dt", full[:, :, 3 * sc :], attended.reshape(n_seq, sc, rows), preferred_element_type=F32
    )
    scale_two = rms_scale(mixed)
    normed_two = ((mixed * scale_two) * gain_two).astype(BF16)

    normed_other = mv.rotate(normed_two, "c")
    parts, sums = [], []
    for j in range(zh):
        results = ffn(
            after(normed_two, *(parts[-1] if j else q_halo)),
            normed_other,
            tangent,
            tangent_other,
            pieces[j],
            starts[j],
        )
        parts.append(results[:4])
        sums.append([ZSum(mv, j, scatter_plane(mv, grad)) for grad in results[4:]])
    out_own, out_other, gn_own, gn_other = (
        sum(four[m].astype(F32) for four in parts) for m in range(4)
    )
    gn_recv = mv.rotate(gn_other.astype(BF16), "c")
    grad_n2 = gn_own + gn_recv.astype(F32)

    grad_mixed, grad_gain_two = norm_back(grad_n2, mixed, scale_two, gain_two)
    grad_mixed = grad_mixed + tangent.astype(F32)
    grad_branch = grad_mixed.astype(BF16)
    grad_att = jnp.einsum(
        "zdc,dt->zct", full[:, :, 3 * sc :], grad_branch, preferred_element_type=F32
    )
    grad_att = grad_att.reshape(inner, rows).astype(BF16)
    delta = jnp.sum((grad_att.astype(F32) * exact).reshape(HEADS, inner // HEADS, rows), axis=1)
    delta = jnp.pad(delta, ((0, 8 - HEADS), (0, 0)))
    delta_top = lax.reduce_precision(delta, 8, 7)
    answers = jnp.concatenate([grad_att, delta_top.astype(BF16), (delta - delta_top).astype(BF16)], 0)
    do_halo = halo(mv, answers)

    dq, near, far = attend_queries(
        off, span, lohi, vec, q, grad_att, lse, delta, own_row, seg_col, kv_halo
    )
    out_recv = mv.rotate(after(out_other.astype(BF16), dq), "c")
    outputs = (mixed + out_own + out_recv.astype(F32)).astype(BF16)
    swaps = [u.swap(dq) for u in sums[0]]
    k_then = after(k, dq, *swaps)
    dk, dv = attend_keys(off, span, lohi, vec, k_then, v, seg_row, own_col, q_halo, do_halo)
    if small:
        dk = after(dk, *[u.inwards() for u in sums[0]])

    sheared = jnp.roll(jnp.sum(near, axis=1), BLK, axis=1)
    grad_table = jnp.dot(sheared, chosen.astype(F32), precision=lax.Precision.HIGHEST).T
    far_sums = jnp.sum(far, axis=(2, 3))
    grad_table = grad_table.at[31].add(far_sums[:, 0]).at[15].add(far_sums[:, 1])

    for groups in sums[1:]:
        swaps = [u.swap(dk) for u in groups]

    split = lambda x: x.reshape(n_seq, sc, rows)
    rows_z = jnp.concatenate([split(dq), split(dk), split(dv)], axis=1)
    grad_normed = jnp.einsum(
        "zdc,zct->dt", full[:, :, : 3 * sc], rows_z, preferred_element_type=F32
    )
    grad_source, grad_gain_one = norm_back(grad_normed, source, scale_one, gain_one)
    input_grad = (grad_mixed + grad_source).astype(BF16)

    g_in = jnp.einsum("dt,zct->zdc", normed, rows_z, preferred_element_type=F32)
    g_out = jnp.einsum("dt,zct->zdc", grad_branch, split(attended), preferred_element_type=F32)
    grads = jnp.concatenate([g_in, g_out], axis=2).reshape(n_seq, n_dp, rw, wide)
    gain_rows = jnp.concatenate(
        [grad_gain_one.reshape(n_dp, rw), grad_gain_two.reshape(n_dp, rw)], axis=1
    )
    widen = lambda x: jnp.broadcast_to(
        jnp.pad(x, ((0, 0), (0, wide - x.shape[1])))[None, :, None, :], (n_seq, n_dp, 1, wide)
    )
    grads = jnp.concatenate(
        [
            grads,
            widen(gain_rows),
            widen(grad_table.reshape(n_dp, -1)),
            jnp.zeros((n_seq, n_dp, rp - rw - 2, wide), F32),
        ],
        axis=2,
    ).astype(BF16)
    if small:
        grads = after(grads, *[u.across() for u in sums[0]])
    own, stages = scatter_small(mv, grads, lambda: [u.home() for u in sums[0]] + swaps if small else [])
    if small:
        for step in (ZSum.inwards, ZSum.across, ZSum.home):
            for u in sums[1]:
                step(u)
    own_ffn = z_totals(mv, sums)

    return (
        outputs.T.reshape(seqs, rows, depth),
        input_grad.T.reshape(seqs, rows, depth),
        own[:rw, :sc],
        own[:rw, sc : 2 * sc],
        own[:rw, 2 * sc : 3 * sc],
        own[:rw, 3 * sc :].T,
        own_ffn[0][0],
        own_ffn[0][1],
        own_ffn[1][0].T,
        own[rw, :rw],
        own[rw, rw : 2 * rw],
        own[rw + 1, : table_row.shape[0]].reshape(rel_table.shape),
    )


def solution(mesh):
    row, col = P("dp", "seq"), P("seq", "dp")
    tokens = P("dp", "seq", None)
    return jax.shard_map(
        partial(on_device, mesh.shape["dp"], mesh.shape["seq"]),
        mesh=mesh,
        in_specs=(tokens, row, tokens, row, row, row, col, row, row, col, P("dp"), P("dp"), P("dp", None)),
        out_specs=(tokens, tokens, row, row, row, col, row, row, col, P("dp"), P("dp"), P("dp", None)),
        check_vma=False,
    )
```

time: 834 us -> 622 us (0.75)
  local copies, waits for them, and re-layouts: 140 us -> 48.6 us
  other arithmetic: 135 us -> 59.2 us
  starting transfers between devices: 137 us -> 90.3 us
  waiting for transfers between devices: 252 us -> 206 us
  Pallas kernels: 132 us -> 164 us
  between operations: 2.6 us -> 16.1 us
    ppermute x35 -> x24, waiting for transfers between devices: 174 us -> 84.6 us  [zperm(): return lax.ppermute(x, 'seq', pairs)]
    ppermute x30 -> x19, waiting for transfers between devices: 78.2 us -> 20.9 us  [rotate(): return lax.ppermute(x, 'dp', pairs)]
    unnamed x186 -> x145, local copies, waits for them, and re-layouts: 46.3 us -> 7.94 us
    ppermute x0 -> x6, waiting for transfers between devices: none -> 38 us  [rotate(): return lax.ppermute(x, 'seq', [(i, (i + 1) % n) for i in range(n)])]
    another operation x37 -> x10, other arithmetic: 44.1 us -> 6.88 us  [ordered(): return jnp.stack([jnp.where(first, x, y), jnp.where(first, y, x)], at)]
    all_gather x0 -> x3, waiting for transfers between devices: none -> 35.6 us  [the longest x1 35.5 us: gather_core(): full = lax.all_gather(w, 'seq')]
    pallas_call x5, Pallas kernels: 132 us -> 164 us  [the longest x2 86 us: ffn(): pl.pallas_call(partial(ffn_kernel, nm, half, len(pieces)), grid_spec=pltp...]
    ppermute x35 -> x24, starting transfers between devices: 103 us -> 72 us  [zperm(): return lax.ppermute(x, 'seq', pairs)]
  transfers between devices with their start and end apart: 65 -> 56, of which waited for: 21 -> 28; matrix products, arithmetic and copies ran while one was open for 33% -> 19% of each run, Pallas kernels for 14% -> 27%
where the time goes in v2:
time: 622 us; the launch traced here: 610 us
  waiting for transfers between devices  206 us (33%)
  Pallas kernels  164 us (26%)
  starting transfers between devices  90.3 us (15%)
  other arithmetic  59.2 us (10%)
  local copies, waits for them, and re-layouts  48.6 us (8%)
  matrix products  26.6 us (4%)
  between operations  16.1 us (3%)
    pallas_call x2, Pallas kernels, ffn(): pl.pallas_call(partial(ffn_kernel, nm, half, len(pieces)), grid_spec=pltp...  86 us
    ppermute x24, waiting for transfers between devices, zperm(): return lax.ppermute(x, 'seq', pairs)  84.6 us
    ppermute x24, starting transfers between devices, zperm(): return lax.ppermute(x, 'seq', pairs)  72 us
    ppermute x6, waiting for transfers between devices, rotate(): return lax.ppermute(x, 'seq', [(i, (i + 1) % n) for i in range(n)])  38 us
    all_gather x1, waiting for transfers between devices, gather_core(): full = lax.all_gather(w, 'seq')  35.5 us
    pallas_call x1, Pallas kernels, attend(): pl.pallas_call(partial(forward_kernel, off, len(kv)), grid=(rows // BLK,)...  26.6 us
    pallas_call x1, Pallas kernels, attend_queries(): pl.pallas_call(partial(query_kernel, off, len(kv)), grid=(rows // BLK,),...  26.4 us
    unnamed x11, waiting for transfers between devices  26.4 us
  transfers between devices with their start and end apart: 56, of which 28 were waited for; matrix products, arithmetic and copies ran while one was open for 19% of the time, Pallas kernels for 27%

profile of v2, /device:TPU:10, one launch (start us, length us, event | category | flops | bytes accessed | tf_op | source)
XLA Modules:
  0.0 610.3 jit_solution(16504507377127735014)
XLA Ops:
  12.5 4.0 collective-permute-done
  23.2 5.7 collective-permute-done.2
  42.6 7.8 %collective-permute-done.4 = bf16[2,2,192,384]{3,2,0,1:T(8,128)(2,1)S(1)} collective-permute-done((bf16[2,2,192,384]{3,2,0,1:T(8,128)(2,1)S(1)}, bf16[2,2,192,384]{3,2,0,1:T(8,128)(2,1)S(1)}, u32[]{:S(2)}, u32[]{:S(2)}) %collective-permute-start.4) | collective-permute-done | bytes 589856 | tf_op jit(solution)/shard_map/ppermute | solution.py:66
  65.6 4.8 fusion.25
  71.5 35.5 %all-gather.9.cloned.1.call-done = bf16[12,184,896]{2,1,0:T(8,128)(2,1)} async-done(((bf16[3,184,896]{2,1,0:T(8,128)(2,1)}), bf16[12,184,896]{2,1,0:T(8,128)(2,1)}) %all-gather.9.cloned.1.call-update) | async-done | bytes 3956752 | tf_op jit(solution)/shard_map/all_gather | solution.py:134
  110.1 4.3 collective-permute-done.18
  120.8 4.9 collective-permute-start.9
  129.7 13.2 %collective-permute-done.9.rest_3_ = bf16[768,512]{1,0:T(8,128)(2,1)S(1)} collective-permute-done((bf16[768,512]{1,0:T(8,128)(2,1)S(1)}, bf16[768,512]{1,0:T(8,128)(2,1)S(1)}, u32[]{:S(2)}, u32[]{:S(2)}) %collective-permute-start.9) | collective-permute-done | bytes 786464 | tf_op jit(solution)/shard_map/ppermute | solution.py:69
  149.3 5.7 collective-permute-start.10
  165.5 12.7 %collective-permute-done.10.rest_0_ = bf16[768,384]{1,0:T(8,128)(2,1)S(1)} collective-permute-done((bf16[768,384]{1,0:T(8,128)(2,1)}, bf16[768,384]{1,0:T(8,128)(2,1)S(1)}, u32[]{:S(2)}, u32[]{:S(2)}) %collective-permute-start.10) | collective-permute-done | bytes 589856 | tf_op jit(solution)/shard_map/ppermute | solution.py:69
  179.0 26.6 %attend.1 = (bf16[384,512]{1,0:T(8,128)(2,1)}, f32[384,512]{1,0:T(8,128)}, f32[8,512]{1,0:T(8,128)}, bf16[32,512]{1,0:T(8,128)(2,1)}) custom-call(s32[2,2]{1,0:T(2,128)} %pad_add_fusion.lohi, f32[6,1024]{1,0:T(8,128)} %fusion.82.vec, bf16[384,512]{1,0:T(8,128)(2,1)} %bitcast.283, s32[2,1,256]{2,1,0:T(1,128)} %bitcast.315, s32[2560,1]{1,0:T(8,128)} %reshape.404.segk, ...), custom_call_target="tpu_custom_call" | custom-call | flops 1000000000 | bytes 8388608 | tf_op jit(solution)/shard_map/attend/pallas_call | solution.py:487
  216.2 8.2 %collective-permute-done.13.rest_3_ = bf16[416,512]{1,0:T(8,128)(2,1)S(1)} collective-permute-done((bf16[416,512]{1,0:T(8,128)(2,1)S(1)}, bf16[416,512]{1,0:T(8,128)(2,1)S(1)}, u32[]{:S(2)}, u32[]{:S(2)}) %collective-permute-start.13) | collective-permute-done | bytes 426016 | tf_op jit(solution)/shard_map/ppermute | solution.py:69
  228.4 7.1 %collective-permute-start.14 = (bf16[416,384]{1,0:T(8,128)(2,1)S(1)}, bf16[416,384]{1,0:T(8,128)(2,1)}, u32[]{:S(2)}, u32[]{:S(2)}) collective-permute-start(bf16[416,384]{1,0:T(8,128)(2,1)S(1)} %get-tuple-element.140), channel_id=1, source_target_pairs={{0,2},{1,3},{4,6},{5,7},{8,10},{9,11},{12,14},{13,15},{16,18},{17,... | collective-permute-start | bytes 958472 | tf_op jit(solution)/shard_map/ppermute | solution.py:69
  239.3 7.6 %collective-permute-done.14.rest_0_ = bf16[416,384]{1,0:T(8,128)(2,1)} collective-permute-done((bf16[416,384]{1,0:T(8,128)(2,1)S(1)}, bf16[416,384]{1,0:T(8,128)(2,1)}, u32[]{:S(2)}, u32[]{:S(2)}) %collective-permute-start.14) | collective-permute-done | bytes 319520 | tf_op jit(solution)/shard_map/ppermute | solution.py:69
  246.9 43.0 %ffn.2 = (bf16[1472,512]{1,0:T(8,128)(2,1)}, bf16[1472,512]{1,0:T(8,128)(2,1)}, bf16[1472,512]{1,0:T(8,128)(2,1)}, bf16[1472,512]{1,0:T(8,128)(2,1)}, bf16[4,2,3...) custom-call(s32[4]{0:T(128)} %iota_multiply_fusion.order, bf16[1472,512]{1,0:T(8,128)(2,1)} %copy-done.4, ...), custom_call_target="tpu_custom_call" | custom-call | flops 1000000000 | bytes 8388608 | tf_op jit(solution)/shard_map/ffn/pallas_call | solution.py:659
  291.0 43.0 %ffn.3 = (bf16[1472,512]{1,0:T(8,128)(2,1)}, bf16[1472,512]{1,0:T(8,128)(2,1)}, bf16[1472,512]{1,0:T(8,128)(2,1)}, bf16[1472,512]{1,0:T(8,128)(2,1)}, bf16[4,2,3...) custom-call(s32[4]{0:T(128)} %iota_multiply_fusion.order, bf16[1472,512]{1,0:T(8,128)(2,1)} %copy-done.4, ...), custom_call_target="tpu_custom_call" | custom-call | flops 1000000000 | bytes 8388608 | tf_op jit(solution)/shard_map/ffn/pallas_call | solution.py:659
  362.8 26.4 %attend_queries.1 = (bf16[384,512]{1,0:T(8,128)(2,1)}, f32[6,8,1024]{2,1,0:T(8,128)}, f32[6,2,8,256]{3,2,1,0:T(8,128)}) custom-call(s32[2,2]{1,0:T(2,128)} %pad_add_fusion.lohi, f32[6,1024]{1,0:T(8,128)} %fusion.82.vec, bf16[384,512]{1,0:T(8,128)(2,1)} %bitcast.284, bf16[384,512]{1,0:T(8,128)(2,1)} %bitcast.282, f32[8,512]{1,0:T(8,128)} %get-tuple-element.87.lse, ...), custom_call_target="tpu_custom_call" | custom-call | flops 1000000000 | bytes 8388608 | tf_op jit(solution)/shard_map/attend_queries/pallas_call | solution.py:508
  404.3 6.2 %collective-permute-start.25 = (bf16[400,384]{1,0:T(8,128)(2,1)S(1)}, bf16[400,384]{1,0:T(8,128)(2,1)}, u32[]{:S(2)}, u32[]{:S(2)}) collective-permute-start(bf16[400,384]{1,0:T(8,128)(2,1)S(1)} %get-tuple-element.142), channel_id=1, source_target_pairs={{0,2},{1,3},{4,6},{5,7},{8,10},{9,11},{12,14},{13,15},{16,18},{17,... | collective-permute-start | bytes 921608 | tf_op jit(solution)/shard_map/ppermute | solution.py:69
  417.7 8.0 %collective-permute-done.28 = bf16[1,184,896]{2,1,0:T(8,128)(2,1)S(1)} collective-permute-done((bf16[1,184,896]{2,1,0:T(8,128)(2,1)S(1)}, bf16[1,184,896]{2,1,0:T(8,128)(2,1)S(1)}, u32[]{:S(2)}, u32[]{:S(2)}) %collective-permute-start.28) | collective-permute-done | bytes 329760 | tf_op jit(solution)/shard_map/ppermute | solution.py:69
  428.6 24.8 %attend_keys.1 = (bf16[384,512]{1,0:T(8,128)(2,1)}, bf16[384,512]{1,0:T(8,128)(2,1)}) custom-call(s32[2,2]{1,0:T(2,128)} %pad_add_fusion.lohi, f32[6,1024]{1,0:T(8,128)} %fusion.82.vec, bf16[384,512]{1,0:T(8,128)(2,1)} %bitcast.290, bf16[384,512]{1,0:T(8,128)(2,1)} %bitcast.291, s32[10,1,256]{2,1,0:T(1,128)} %reshape.374.segq, s32[512,1]{1,0:T(8,128)} %copy.107.segk, ...), custom_call_target="tpu_custom_call" | custom-call | flops 1000000000 | bytes 8388608 | tf_op jit(solution)/shard_map/attend_keys/pallas_call | solution.py:542
  460.1 4.2 fusion.17
  467.0 6.8 %copy.108 = bf16[4,1472,384]{2,1,0:T(8,128)(2,1)} copy(bf16[4,1472,384]{1,2,0:T(8,128)(2,1)} %pad_maximum_fusion.1) | data formatting | bytes 9043968 | tf_op jit(solution)/shard_map/concatenate | solution.py:860
  483.5 23.7 %reduce-scatter.17.cloned.1.call-done = bf16[1,2,368,896]{3,2,1,0:T(8,128)(2,1)} async-done(((bf16[4,2,368,896]{3,2,1,0:T(8,128)(2,1)}), bf16[1,2,368,896]{3,2,1,0:T(8,128)(2,1)}) %reduce-scatter.17.cloned.1.call-update) | async-done | bytes 1318928
  512.7 4.2 fusion.29
  517.2 4.7 collective-permute-start.32
  522.7 4.1 collective-permute-start.47
  530.7 5.1 collective-permute-done.32
  540.1 6.5 %collective-permute-done.43 = bf16[2,184,896]{2,1,0:T(8,128)(2,1)S(1)} collective-permute-done((bf16[2,184,896]{2,1,0:T(8,128)(2,1)S(1)}, bf16[2,184,896]{2,1,0:T(8,128)(2,1)S(1)}, u32[]{:S(2)}, u32[]{:S(2)}) %collective-permute-start.43) | collective-permute-done | bytes 659488 | tf_op jit(solution)/shard_map/ppermute | solution.py:69
  546.8 7.7 %collective-permute-start.44 = (bf16[2,184,896]{2,1,0:T(8,128)(2,1)S(1)}, bf16[2,184,896]{2,1,0:T(8,128)(2,1)S(1)}, u32[]{:S(2)}, u32[]{:S(2)}) collective-permute-start(bf16[2,184,896]{2,1,0:T(8,128)(2,1)S(1)} %add_convert_fusion.4), channel_id=1, source_target_pairs={{1,2},{2,1},{5,6},{6,5},{9,10},{10,9},{13,14},{14,13},{17,18},{18,... | collective-permute-start | bytes 1978376 | tf_op jit(solution)/shard_map/ppermute | solution.py:69
  557.0 11.8 %collective-permute-done.44 = bf16[2,184,896]{2,1,0:T(8,128)(2,1)S(1)} collective-permute-done((bf16[2,184,896]{2,1,0:T(8,128)(2,1)S(1)}, bf16[2,184,896]{2,1,0:T(8,128)(2,1)S(1)}, u32[]{:S(2)}, u32[]{:S(2)}) %collective-permute-start.44) | collective-permute-done | bytes 659488 | tf_op jit(solution)/shard_map/ppermute | solution.py:69
  574.5 15.2 %collective-permute-done.40 = bf16[192,384]{1,0:T(8,128)(2,1)S(1)} collective-permute-done((bf16[192,384]{1,0:T(8,128)(2,1)S(1)}, bf16[192,384]{1,0:T(8,128)(2,1)S(1)}, u32[]{:S(2)}, u32[]{:S(2)}) %collective-permute-start.40) | collective-permute-done | bytes 147488 | tf_op jit(solution)/shard_map/ppermute | solution.py:54
  590.1 5.4 collective-permute-done.41
  (377 shorter events, 195.1 us)
Async XLA Ops:
  7.2 99.8 %all-gather.9.cloned.1.call-start = ((), (), s32[]{:S(2)}) async-start(), calls=%async_computation.6 | async-start | bytes 4945920 | tf_op jit(solution)/shard_map/all_gather | solution.py:134
  30.9 216.0 %all-gather.5.cloned.1.call-start = ((), (), s32[]{:S(2)}) async-start(), calls=%async_computation.4 | async-start | bytes 9891840 | tf_op jit(solution)/shard_map/all_gather | solution.py:758
  53.7 56.4 %collective-permute-start.17 = (bf16[1472,512]{1,0:T(8,128)(2,1)S(1)}, bf16[1472,512]{1,0:T(8,128)(2,1)S(1)}, u32[]{:S(2)}, u32[]{:S(2)}) collective-permute-start(bf16[1472,512]{1,0:T(8,128)(2,1)S(1)} %bitcast.263), channel_id=1, source_target_pairs={{0,4},{4,0},{8,12},{12,8},{16,20},{20,16},{24,28},{28,24},{1,5},{5... | collective-permute-start | bytes 4521992 | tf_op jit(solution)/shard_map/ppermute | solution.py:66
  118.9 172.2 %all-gather.7.cloned.1.call-start = ((), (), s32[]{:S(2)}) async-start(), calls=%async_computation.5 | async-start | bytes 9891840 | tf_op jit(solution)/shard_map/all_gather | solution.py:758
  120.4 276.8 %reduce-scatter.15.cloned.1.call-start = ((), (), s32[]{:S(2)}) async-start(), calls=%async_computation.8 | async-start | bytes 3297280
  120.8 22.2 %collective-permute-start.9 = (bf16[768,512]{1,0:T(8,128)(2,1)S(1)}, bf16[768,512]{1,0:T(8,128)(2,1)S(1)}, u32[]{:S(2)}, u32[]{:S(2)}) collective-permute-start(bf16[768,512]{1,0:T(8,128)(2,1)S(1)} %pad_maximum_fusion.6.rest_2_), channel_id=1, source_target_pairs={{1,0},{2,1},{3,2},{5,4},{6,5},{7,6},{9,8},{10,9},{11,10},{13,12},{... | collective-permute-start | bytes 2359304 | tf_op jit(solution)/shard_map/ppermute | solution.py:69
  125.6 21.2 %collective-permute-start.8 = (bf16[768,512]{1,0:T(8,128)(2,1)S(1)}, bf16[768,512]{1,0:T(8,128)(2,1)S(1)}, u32[]{:S(2)}, u32[]{:S(2)}) collective-permute-start(bf16[768,512]{1,0:T(8,128)(2,1)S(1)} %pad_maximum_fusion.6.rest_2_), channel_id=1, source_target_pairs={{0,1},{1,2},{2,3},{4,5},{5,6},{6,7},{8,9},{9,10},{10,11},{12,13},{... | collective-permute-start | bytes 2359304 | tf_op jit(solution)/shard_map/ppermute | solution.py:69
  148.0 17.4 %collective-permute-start.11 = (bf16[768,384]{1,0:T(8,128)(2,1)}, bf16[768,384]{1,0:T(8,128)(2,1)S(1)}, u32[]{:S(2)}, u32[]{:S(2)}) collective-permute-start(bf16[768,384]{1,0:T(8,128)(2,1)} %get-tuple-element.133), channel_id=1, source_target_pairs={{2,0},{3,1},{6,4},{7,5},{10,8},{11,9},{14,12},{15,13},{18,16},{19,... | collective-permute-start | bytes 1769480 | tf_op jit(solution)/shard_map/ppermute | solution.py:69
  149.3 28.9 %collective-permute-start.10 = (bf16[768,384]{1,0:T(8,128)(2,1)}, bf16[768,384]{1,0:T(8,128)(2,1)S(1)}, u32[]{:S(2)}, u32[]{:S(2)}) collective-permute-start(bf16[768,384]{1,0:T(8,128)(2,1)} %get-tuple-element.134), channel_id=1, source_target_pairs={{0,2},{1,3},{4,6},{5,7},{8,10},{9,11},{12,14},{13,15},{16,18},{17,... | collective-permute-start | bytes 1769480 | tf_op jit(solution)/shard_map/ppermute | solution.py:69
  210.2 36.7 %collective-permute-start.16 = (bf16[1472,512]{1,0:T(8,128)(2,1)S(1)}, bf16[1472,512]{1,0:T(8,128)(2,1)}, u32[]{:S(2)}, u32[]{:S(2)}) collective-permute-start(bf16[1472,512]{1,0:T(8,128)(2,1)S(1)} %multiply_convert_fusion.na.nat), channel_id=1, source_target_pairs={{0,4},{4,0},{8,12},{12,8},{16,20},{20,16},{24,28},{28,24},{1,5},{5... | collective-permute-start | bytes 4521992 | tf_op jit(solution)/shard_map/ppermute | solution.py:66
  228.4 18.5 %collective-permute-start.14 = (bf16[416,384]{1,0:T(8,128)(2,1)S(1)}, bf16[416,384]{1,0:T(8,128)(2,1)}, u32[]{:S(2)}, u32[]{:S(2)}) collective-permute-start(bf16[416,384]{1,0:T(8,128)(2,1)S(1)} %get-tuple-element.140), channel_id=1, source_target_pairs={{0,2},{1,3},{4,6},{5,7},{8,10},{9,11},{12,14},{13,15},{16,18},{17,... | collective-permute-start | bytes 958472 | tf_op jit(solution)/shard_map/ppermute | solution.py:69
  289.9 108.9 %reduce-scatter.13.cloned.1.call-start = ((), (), s32[]{:S(2)}) async-start(), calls=%async_computation.7 | async-start | bytes 6594560
  290.5 193.0 %reduce-scatter.19.cloned.1.call-start = ((), (), s32[]{:S(2)}) async-start(), calls=%async_computation.10 | async-start | bytes 3297280
  334.1 173.1 %reduce-scatter.17.cloned.1.call-start = ((), (), s32[]{:S(2)}) async-start(), calls=%async_computation.9 | async-start | bytes 6594560
  357.0 44.9 %collective-permute-start.24 = (bf16[400,512]{1,0:T(8,128)(2,1)}, bf16[400,512]{1,0:T(8,128)(2,1)}, u32[]{:S(2)}, u32[]{:S(2)}) collective-permute-start(bf16[400,512]{1,0:T(8,128)(2,1)} %pad_maximum_fusion.12.rest_7_), channel_id=1, source_target_pairs={{1,0},{2,1},{3,2},{5,4},{6,5},{7,6},{9,8},{10,9},{11,10},{13,12},{... | collective-permute-start | bytes 1228808 | tf_op jit(solution)/shard_map/ppermute | solution.py:69
  358.9 43.0 %collective-permute-start.23 = (bf16[400,512]{1,0:T(8,128)(2,1)}, bf16[400,512]{1,0:T(8,128)(2,1)}, u32[]{:S(2)}, u32[]{:S(2)}) collective-permute-start(bf16[400,512]{1,0:T(8,128)(2,1)} %pad_maximum_fusion.12.rest_7_), channel_id=1, source_target_pairs={{0,1},{1,2},{2,3},{4,5},{5,6},{6,7},{8,9},{9,10},{10,11},{12,13},{... | collective-permute-start | bytes 1228808 | tf_op jit(solution)/shard_map/ppermute | solution.py:69
  391.3 22.9 %collective-permute-start.20 = (bf16[1472,512]{1,0:T(8,128)(2,1)}, bf16[1472,512]{1,0:T(8,128)(2,1)}, u32[]{:S(2)}, u32[]{:S(2)}) collective-permute-start(bf16[1472,512]{1,0:T(8,128)(2,1)} %add_convert_fusion.2), channel_id=1, source_target_pairs={{0,4},{4,0},{8,12},{12,8},{16,20},{20,16},{24,28},{28,24},{1,5},{5... | collective-permute-start | bytes 4521992 | tf_op jit(solution)/shard_map/ppermute | solution.py:66
  403.0 24.9 %collective-permute-start.26 = (bf16[400,384]{1,0:T(8,128)(2,1)S(1)}, bf16[400,384]{1,0:T(8,128)(2,1)S(1)}, u32[]{:S(2)}, u32[]{:S(2)}) collective-permute-start(bf16[400,384]{1,0:T(8,128)(2,1)S(1)} %get-tuple-element.141), channel_id=1, source_target_pairs={{2,0},{3,1},{6,4},{7,5},{10,8},{11,9},{14,12},{15,13},{18,16},{19,... | collective-permute-start | bytes 921608 | tf_op jit(solution)/shard_map/ppermute | solution.py:69
  404.3 23.6 %collective-permute-start.25 = (bf16[400,384]{1,0:T(8,128)(2,1)S(1)}, bf16[400,384]{1,0:T(8,128)(2,1)}, u32[]{:S(2)}, u32[]{:S(2)}) collective-permute-start(bf16[400,384]{1,0:T(8,128)(2,1)S(1)} %get-tuple-element.142), channel_id=1, source_target_pairs={{0,2},{1,3},{4,6},{5,7},{8,10},{9,11},{12,14},{13,15},{16,18},{17,... | collective-permute-start | bytes 921608 | tf_op jit(solution)/shard_map/ppermute | solution.py:69
  412.7 40.7 %collective-permute-start.27 = (bf16[2,184,896]{2,1,0:T(8,128)(2,1)S(1)}, bf16[2,184,896]{2,1,0:T(8,128)(2,1)}, u32[]{:S(2)}, u32[]{:S(2)}) collective-permute-start(bf16[2,184,896]{2,1,0:T(8,128)(2,1)S(1)} %bitcast_select_fusion.3), channel_id=1, source_target_pairs={{0,1},{3,2},{4,5},{7,6},{8,9},{11,10},{12,13},{15,14},{16,17},{19,... | collective-permute-start | bytes 1978376 | tf_op jit(solution)/shard_map/ppermute | solution.py:69
  425.8 51.2 %collective-permute-start.30 = (bf16[1,184,896]{2,1,0:T(8,128)(2,1)S(1)}, bf16[1,184,896]{2,1,0:T(8,128)(2,1)S(1)}, u32[]{:S(2)}, u32[]{:S(2)}) collective-permute-start(bf16[1,184,896]{2,1,0:T(8,128)(2,1)S(1)} %add_convert_fusion.10), channel_id=1, source_target_pairs={{1,2},{2,1},{5,6},{6,5},{9,10},{10,9},{13,14},{14,13},{17,18},{18,... | collective-permute-start | bytes 989192 | tf_op jit(solution)/shard_map/ppermute | solution.py:69
  454.7 22.3 %collective-permute-start.29 = (bf16[2,184,896]{2,1,0:T(8,128)(2,1)S(1)}, bf16[2,184,896]{2,1,0:T(8,128)(2,1)S(1)}, u32[]{:S(2)}, u32[]{:S(2)}) collective-permute-start(bf16[2,184,896]{2,1,0:T(8,128)(2,1)S(1)} %add_convert_fusion.6), channel_id=1, source_target_pairs={{1,2},{2,1},{5,6},{6,5},{9,10},{10,9},{13,14},{14,13},{17,18},{18,... | collective-permute-start | bytes 1978376 | tf_op jit(solution)/shard_map/ppermute | solution.py:69
  480.1 48.1 %collective-permute-start.31 = (bf16[4,2,2,192,384]{4,3,2,1,0:T(8,128)(2,1)}, bf16[4,2,2,192,384]{4,3,2,1,0:T(8,128)(2,1)}, u32[]{:S(2)}, u32[]{:S(2)}) collective-permute-start(bf16[4,2,2,192,384]{4,3,2,1,0:T(8,128)(2,1)} %dynamic-slice_bitcast_fusion), channel_id=1, source_target_pairs={{0,4},{4,0},{8,12},{12,8},{16,20},{20,16},{24,28},{28,24},{1,5},{5... | collective-permute-start | bytes 7077896 | tf_op jit(solution)/shard_map/ppermute | solution.py:66
  481.4 49.3 %collective-permute-start.33 = (bf16[1,184,896]{2,1,0:T(8,128)(2,1)S(1)}, bf16[1,184,896]{2,1,0:T(8,128)(2,1)}, u32[]{:S(2)}, u32[]{:S(2)}) collective-permute-start(bf16[1,184,896]{2,1,0:T(8,128)(2,1)S(1)} %add_convert_fusion.9), channel_id=1, source_target_pairs={{1,0},{3,2},{5,4},{7,6},{9,8},{11,10},{13,12},{15,14},{17,16},{19,... | collective-permute-start | bytes 989192 | tf_op jit(solution)/shard_map/ppermute | solution.py:69
  509.4 17.4 %collective-permute-start.34 = (bf16[2,184,896]{2,1,0:T(8,128)(2,1)S(1)}, bf16[2,184,896]{2,1,0:T(8,128)(2,1)S(1)}, u32[]{:S(2)}, u32[]{:S(2)}) collective-permute-start(bf16[2,184,896]{2,1,0:T(8,128)(2,1)S(1)} %dynamic-slice_bitcast_fusion.1), channel_id=1, source_target_pairs={{0,4},{4,0},{8,12},{12,8},{16,20},{20,16},{24,28},{28,24},{1,5},{5... | collective-permute-start | bytes 1978376 | tf_op jit(solution)/shard_map/ppermute | solution.py:66
  517.2 18.7 %collective-permute-start.32 = (bf16[2,184,896]{2,1,0:T(8,128)(2,1)S(1)}, bf16[2,184,896]{2,1,0:T(8,128)(2,1)S(1)}, u32[]{:S(2)}, u32[]{:S(2)}) collective-permute-start(bf16[2,184,896]{2,1,0:T(8,128)(2,1)S(1)} %add_convert_fusion.5), channel_id=1, source_target_pairs={{1,0},{3,2},{5,4},{7,6},{9,8},{11,10},{13,12},{15,14},{17,16},{19,... | collective-permute-start | bytes 1978376 | tf_op jit(solution)/shard_map/ppermute | solution.py:69
  527.0 19.7 %collective-permute-start.43 = (bf16[2,184,896]{2,1,0:T(8,128)(2,1)S(1)}, bf16[2,184,896]{2,1,0:T(8,128)(2,1)S(1)}, u32[]{:S(2)}, u32[]{:S(2)}) collective-permute-start(bf16[2,184,896]{2,1,0:T(8,128)(2,1)S(1)} %bitcast_select_fusion), channel_id=1, source_target_pairs={{0,1},{3,2},{4,5},{7,6},{8,9},{11,10},{12,13},{15,14},{16,17},{19,... | collective-permute-start | bytes 1978376 | tf_op jit(solution)/shard_map/ppermute | solution.py:69
  536.1 18.4 %collective-permute-start.38 = (bf16[2,2,192,384]{3,2,1,0:T(8,128)(2,1)S(1)}, bf16[2,2,192,384]{3,2,1,0:T(8,128)(2,1)S(1)}, u32[]{:S(2)}, u32[]{:S(2)}) collective-permute-start(bf16[2,2,192,384]{3,2,1,0:T(8,128)(2,1)S(1)} %dynamic-slice_bitcast_fusion.3), channel_id=1, source_target_pairs={{0,8},{4,12},{8,0},{12,4},{16,24},{20,28},{24,16},{28,20},{1,9},{5... | collective-permute-start | bytes 1769480 | tf_op jit(solution)/shard_map/ppermute | solution.py:66
  537.0 35.5 %collective-permute-start.48 = (bf16[1,184,896]{2,1,0:T(8,128)(2,1)S(1)}, bf16[1,184,896]{2,1,0:T(8,128)(2,1)S(1)}, u32[]{:S(2)}, u32[]{:S(2)}) collective-permute-start(bf16[1,184,896]{2,1,0:T(8,128)(2,1)S(1)} %add_convert_fusion.7), channel_id=1, source_target_pairs={{0,1},{2,3},{4,5},{6,7},{8,9},{10,11},{12,13},{14,15},{16,17},{18,... | collective-permute-start | bytes 989192 | tf_op jit(solution)/shard_map/ppermute | solution.py:69
  546.8 22.0 %collective-permute-start.44 = (bf16[2,184,896]{2,1,0:T(8,128)(2,1)S(1)}, bf16[2,184,896]{2,1,0:T(8,128)(2,1)S(1)}, u32[]{:S(2)}, u32[]{:S(2)}) collective-permute-start(bf16[2,184,896]{2,1,0:T(8,128)(2,1)S(1)} %add_convert_fusion.4), channel_id=1, source_target_pairs={{1,2},{2,1},{5,6},{6,5},{9,10},{10,9},{13,14},{14,13},{17,18},{18,... | collective-permute-start | bytes 1978376 | tf_op jit(solution)/shard_map/ppermute | solution.py:69
  569.1 20.7 %collective-permute-start.45 = (bf16[2,184,896]{2,1,0:T(8,128)(2,1)S(1)}, bf16[2,184,896]{2,1,0:T(8,128)(2,1)S(1)}, u32[]{:S(2)}, u32[]{:S(2)}) collective-permute-start(bf16[2,184,896]{2,1,0:T(8,128)(2,1)S(1)} %add_convert_fusion.3), channel_id=1, source_target_pairs={{0,1},{2,3},{4,5},{6,7},{8,9},{10,11},{12,13},{14,15},{16,17},{18,... | collective-permute-start | bytes 1978376 | tf_op jit(solution)/shard_map/ppermute | solution.py:69
  570.7 19.0 %collective-permute-start.40 = (bf16[192,384]{1,0:T(8,128)(2,1)S(1)}, bf16[192,384]{1,0:T(8,128)(2,1)S(1)}, u32[]{:S(2)}, u32[]{:S(2)}) collective-permute-start(bf16[192,384]{1,0:T(8,128)(2,1)S(1)} %fusion.50), channel_id=1, source_target_pairs={{0,1},{1,2},{2,3},{3,0},{4,5},{5,6},{6,7},{7,4},{8,9},{9,10},{10,1... | collective-permute-start | bytes 442376 | tf_op jit(solution)/shard_map/ppermute | solution.py:54
  (91 other events, 979.9 us)
Sparse Core Ops, SparseCore 0:
  31.1 75.9 all-gather.8
  119.0 84.5 all-gather.4
  205.5 83.6 all-gather.6
  292.0 41.7 reduce-scatter.14
  337.0 61.7 reduce-scatter.12
  401.9 40.4 reduce-scatter.18
  445.4 61.6 reduce-scatter.16
